TPU v7x, 256 devices: a whole 4x4x8 slice. The times are simulated.
256 devices in a mesh: seq: 32 (over y, z_lo, core), tensor: 8 (over x, z_hi).
Axes of the slice: x: 4, y: 4, z: 8 (z_hi: 2, z_lo: 4; z = z_hi * 4 + z_lo), core: 2. Of those that a mesh axis runs over, the one named last changes fastest.
Arguments:
- features: bfloat16 [4, 40, 64, 512], P(None, 'tensor', 'seq'), may hold values from -6 to 6
- conv_weight: bfloat16 [3, 3, 3, 512, 16], replicated, may hold values from -0.0546875 to 0.0546875
- conv_bias: float32 [16], replicated, may hold values from -4 to 4
- embed_weight: bfloat16 [16, 5120], replicated, may hold values from -1.5 to 1.5
- position_table: bfloat16 [10240, 5120], P('seq'), may hold values from -6 to 6
- norm_gain: bfloat16 [5120], replicated, may hold values from 0.099609375 to 1.8984375
- qkv_weight: bfloat16 [5120, 6144], P('seq', 'tensor'), may hold values from -1 to 1
- page_owner: int32 [1280], P('seq'), may hold values from 0 to 31, as said below
- page_slot: int32 [1280], P('seq'), may hold values from 0 to 39, as said below
Outputs:
- attention: bfloat16 [10240, 4096], P('seq', 'tensor')
- kv_cache: bfloat16 [1280, 8, 2, 1024], P('seq', None, None, 'tensor')
Inputs may be any that keep to these rules, and one draw needn't show every extreme that they name: `page_owner`: of the 40 pages of one index of seq, at most 3 have the same owner, and exactly 3 for some owner. Every owner keeps exactly 40 pages. `page_slot`: the pages of one owner use each slot 0 to 39 once.
All inputs are finite; a program needn't handle non-finite values.
Results may differ from a plain program's by a relative error of at most 0.0084.
Values may be sent and summed in bfloat16 or wider, within the bound.
No kernel may reach another device: no remote copies, remote signals or barrier semaphores. Data moves between devices by JAX's collectives and lax.ppermute only.
A program may use at most 128 MiB of HBM per device.

v0:
```python
import functools

import jax
import jax.numpy as jnp
import numpy as np
from jax import lax
from jax.experimental import pallas as pl
from jax.experimental.pallas import tpu as pltpu
from jax.sharding import PartitionSpec as P

HD = 128
PAGE = 8
GROUP = 4
LAT = 16
BLK = 320
PAGES = 40
MOST = 3
SEQ = 32
ROWS = 5
COLS = 2
FRAMES = 4
EXT = (ROWS + 2) * (COLS + 2)
TOK = 384
TILE = 256
QROWS = GROUP * BLK
STATE = HD + 8
VMEM = 24 * 1024 * 1024


def params(**extra):
    return pltpu.CompilerParams(vmem_limit_bytes=VMEM, **extra)


def cost(blocks):
    scores = blocks * 2 * QROWS * BLK
    return pl.CostEstimate(flops=4 * HD * scores, bytes_accessed=3 << 20, transcendentals=scores)


def roll_lanes(value, shift):
    shift = shift % value.shape[1]
    return pltpu.roll(value, shift, 1) if shift else value


def conv_kernel(feat_ref, weight_ref, out_ref, grid_ref):
    grid_ref[...] = jnp.zeros_like(grid_ref)
    for frame in range(FRAMES):
        for row in range(ROWS):
            start = frame * EXT + (row + 1) * (COLS + 2) + 1
            value = feat_ref[frame, row].astype(jnp.float32)
            grid_ref[start : start + COLS, :] = value / (1.0 + jnp.exp(-value))
    active = grid_ref[...].astype(jnp.bfloat16)
    product = lax.dot_general(
        weight_ref[...], active, (((1,), (1,)), ((), ())), preferred_element_type=jnp.float32
    )
    lane = lax.broadcasted_iota(jnp.int32, (LAT, 128), 1)
    total = jnp.zeros((LAT, 128), jnp.float32)
    for time in range(3):
        part = jnp.zeros((LAT, 128), jnp.float32)
        for row in range(3):
            for col in range(3):
                index = (time * 3 + row) * 3 + col
                piece = product[index * LAT : (index + 1) * LAT, :]
                part = part + roll_lanes(piece, -((row - 1) * (COLS + 2) + col - 1))
        delay = (2 - time) * EXT
        if delay:
            part = jnp.where(lane >= delay, roll_lanes(part, delay), 0.0)
        total = total + part
    padded = jnp.concatenate([total, jnp.zeros((128 - LAT, 128), jnp.float32)], axis=0)
    out_ref[...] = jnp.transpose(padded)[:, :LAT]


def partial_latents(features, conv_weight):
    weight = jnp.transpose(conv_weight, (0, 1, 2, 4, 3)).reshape(-1, conv_weight.shape[3])
    return pl.pallas_call(
        conv_kernel,
        out_shape=jax.ShapeDtypeStruct((128, LAT), jnp.float32),
        scratch_shapes=[pltpu.VMEM((128, features.shape[-1]), jnp.float32)],
        compiler_params=params(),
        name="conv",
    )(features, weight)


def split_three(value):
    high = value.astype(jnp.bfloat16)
    rest = value - high.astype(jnp.float32)
    middle = rest.astype(jnp.bfloat16)
    low = (rest - middle.astype(jnp.float32)).astype(jnp.bfloat16)
    return high, middle, low


def place_kernel(offset_ref, parts_ref, token_ref, out_ref):
    count = parts_ref.shape[0]
    token = lax.broadcasted_iota(jnp.int32, (TOK, count), 0) - offset_ref[0] * BLK
    pick = jnp.where(token == token_ref[...], 1.0, 0.0).astype(jnp.bfloat16)
    total = jnp.zeros((LAT, TOK), jnp.float32)
    for part in reversed(split_three(parts_ref[...])):
        total = total + lax.dot_general(
            part, pick, (((0,), (1,)), ((), ())), preferred_element_type=jnp.float32
        )
    out_ref[...] = total


def place_table():
    row = np.arange(ROWS + 2).reshape(1, -1, 1) - 1
    col = np.arange(COLS + 2).reshape(1, 1, -1) - 1
    width = np.arange(SEQ).reshape(-1, 1, 1) * COLS + col
    inside = (width >= 0) & (width < SEQ * COLS)
    token = np.where(inside, row * SEQ * COLS + width, -(1 << 20))
    return token.astype(np.int32).reshape(1, SEQ * EXT)


def place_latents(parts, offset):
    return pl.pallas_call(
        place_kernel,
        in_specs=[pl.BlockSpec(memory_space=pltpu.SMEM)]
        + [pl.BlockSpec(memory_space=pltpu.VMEM)] * 2,
        out_shape=jax.ShapeDtypeStruct((LAT, TOK), jnp.float32),
        compiler_params=params(),
        name="place",
    )(offset.reshape(1), parts, jnp.asarray(place_table()))


def hidden_kernel(latent_ref, embed_ref, table_ref, gain_ref, out_ref, hid_ref, sq_ref):
    step = pl.program_id(0)
    width = table_ref.shape[1]
    latent = latent_ref[...][:, :BLK]
    latent = jnp.concatenate(split_three(latent), axis=0)
    embed = embed_ref[...]
    hidden = lax.dot_general(
        latent,
        jnp.concatenate([embed, embed, embed], axis=0),
        (((0,), (0,)), ((), ())),
        preferred_element_type=jnp.float32,
    ) + table_ref[...].astype(jnp.float32)
    hid_ref[step] = hidden
    squares = jnp.zeros((BLK, 128), jnp.float32)
    for lane in range(0, width, 128):
        piece = hidden[:, lane : lane + 128]
        squares = squares + piece * piece

    @pl.when(step == 0)
    def _():
        sq_ref[...] = squares

    @pl.when(step > 0)
    def _():
        sq_ref[...] += squares

    @pl.when(step == pl.num_programs(0) - 1)
    def _():
        count = hid_ref.shape[0]
        mean = jnp.sum(sq_ref[...], axis=1, keepdims=True) / (count * width)
        factor = lax.rsqrt(mean + 1e-05)
        for tile in range(count):
            gain = gain_ref[:, tile * width : (tile + 1) * width].astype(jnp.float32)
            normed = hid_ref[tile] * factor * gain
            out_ref[:, tile * width : (tile + 1) * width] = normed.astype(jnp.bfloat16)


def normed_hidden(latent, embed_weight, position_table, gain):
    depth = position_table.shape[1]
    steps = 8
    width = depth // steps
    return pl.pallas_call(
        hidden_kernel,
        grid=(steps,),
        in_specs=[
            pl.BlockSpec((LAT, TOK), lambda i: (0, 0)),
            pl.BlockSpec((LAT, width), lambda i: (0, i)),
            pl.BlockSpec((BLK, width), lambda i: (0, i)),
            pl.BlockSpec((1, depth), lambda i: (0, 0)),
        ],
        out_specs=pl.BlockSpec((BLK, depth), lambda i: (0, 0)),
        out_shape=jax.ShapeDtypeStruct((BLK, depth), jnp.bfloat16),
        scratch_shapes=[
            pltpu.VMEM((steps, BLK, width), jnp.float32),
            pltpu.VMEM((BLK, 128), jnp.float32),
        ],
        compiler_params=params(dimension_semantics=("arbitrary",)),
        name="hidden",
    )(latent, embed_weight, position_table, gain)


def attend_block(masked, partner_full, keys, values, q_ref, state_ref):
    scale = 1.4426950408889634 / HD**0.5
    tiles = 2 * QROWS // TILE

    def score(tile):
        return lax.dot_general(
            keys,
            q_ref[tile * TILE : (tile + 1) * TILE, :],
            (((1,), (1,)), ((), ())),
            preferred_element_type=jnp.float32,
        )

    upcoming = score(0)
    for tile in range(tiles):
        scores = upcoming
        if tile + 1 < tiles:
            upcoming = score(tile + 1)
        cut = slice(tile * TILE, (tile + 1) * TILE)
        allowed = None
        if masked:
            key = lax.broadcasted_iota(jnp.int32, scores.shape, 0)
            query = tile * TILE + lax.broadcasted_iota(jnp.int32, (1, TILE), 1)
            if tile * TILE >= QROWS:
                query = jnp.where(partner_full, BLK, -1) + 0 * query
            else:
                for head in range(GROUP - 1, 0, -1):
                    query = jnp.where(query >= head * BLK, query - head * BLK, query)
            allowed = key <= query
            scores = jnp.where(allowed, scores, -1e30)
        peak = jnp.max(scores, axis=0, keepdims=True)
        if masked:
            best = peak
        else:
            old = state_ref[HD : HD + 1, cut]
            best = jnp.maximum(old, peak)
            factor = jnp.exp2((old - best) * scale)
        weights = jnp.exp2((scores - best) * scale)
        if masked:
            weights = jnp.where(allowed, weights, 0.0)
        total = jnp.sum(weights, axis=0, keepdims=True)
        summed = lax.dot_general(
            values,
            weights.astype(jnp.bfloat16),
            (((0,), (0,)), ((), ())),
            preferred_element_type=jnp.float32,
        )
        if not masked:
            total = total + state_ref[HD + 1 : HD + 2, cut] * factor
            summed = summed + state_ref[:HD, cut] * factor
        state_ref[HD : HD + 1, cut] = best
        state_ref[HD + 1 : HD + 2, cut] = total
        state_ref[:HD, cut] = summed


def attend_rolled(keys, values, q_ref, state_ref, score_ref):
    scale = 1.4426950408889634 / HD**0.5
    tiles = 2 * QROWS // TILE
    rows = keys.shape[0]

    def score(tile, slot):
        start = pl.multiple_of(jnp.minimum(tile, tiles - 1) * TILE, TILE)
        score_ref[slot, :rows, :] = lax.dot_general(
            keys,
            q_ref[pl.ds(start, TILE), :],
            (((1,), (1,)), ((), ())),
            preferred_element_type=jnp.float32,
        )

    def update(tile, slot):
        cut = pl.ds(pl.multiple_of(tile * TILE, TILE), TILE)
        scores = score_ref[slot, :rows, :]
        old = state_ref[HD : HD + 1, cut]
        best = jnp.maximum(old, jnp.max(scores, axis=0, keepdims=True))
        factor = jnp.exp2((old - best) * scale)
        weights = jnp.exp2((scores - best) * scale)
        total = jnp.sum(weights, axis=0, keepdims=True)
        summed = lax.dot_general(
            values,
            weights.astype(jnp.bfloat16),
            (((0,), (0,)), ((), ())),
            preferred_element_type=jnp.float32,
        )
        state_ref[HD : HD + 1, cut] = best
        state_ref[HD + 1 : HD + 2, cut] = total + state_ref[HD + 1 : HD + 2, cut] * factor
        state_ref[:HD, cut] = summed + state_ref[:HD, cut] * factor

    score(0, 0)

    def body(pair, carry):
        score(2 * pair + 1, 1)
        update(2 * pair, 0)
        score(2 * pair + 2, 0)
        update(2 * pair + 1, 1)
        return carry

    lax.fori_loop(0, tiles // 2, body, 0)


def first_kernel(core_ref, own_ref, pair_ref, kv_ref, state_ref, q_ref):
    for index, ref in enumerate((own_ref, pair_ref)):
        for head in range(GROUP):
            start = (index * GROUP + head) * BLK
            q_ref[start : start + BLK, :] = ref[:, head * HD : (head + 1) * HD]
    state_ref[HD + 2 :, :] = jnp.zeros((STATE - HD - 2, 2 * QROWS), jnp.float32)
    attend_block(True, core_ref[0] == 0, kv_ref[:, :HD], kv_ref[:, HD:], q_ref, state_ref)


def attend_first(core, own, pair, kv):
    return pl.pallas_call(
        first_kernel,
        in_specs=[pl.BlockSpec(memory_space=pltpu.SMEM)]
        + [pl.BlockSpec(memory_space=pltpu.VMEM)] * 3,
        out_shape=(
            jax.ShapeDtypeStruct((STATE, 2 * QROWS), jnp.float32),
            jax.ShapeDtypeStruct((2 * QROWS, HD), jnp.bfloat16),
        ),
        compiler_params=params(),
        cost_estimate=cost(1),
        name="first",
    )(core.reshape(1), own, pair, kv)


def more_kernel(count, split, flag_ref, q_ref, state_ref, *rest):
    arrays, rest = rest[:count], rest[count:]
    if split:
        own_out_ref, pair_out_ref, held_ref, sems, score_ref, work_ref = rest
    else:
        work_ref, held_ref, sems, score_ref = rest
    copies = []
    for index, array in enumerate(arrays):
        unit = array.shape[0]
        held = held_ref.at[pl.ds(index * unit, unit), :]
        copies.append(pltpu.make_async_copy(array, held, sems.at[index]))
        copies[-1].start()
    work_ref[...] = state_ref[...]
    for copy in copies:
        copy.wait()

    every = jnp.int32(unit == BLK)
    for index in range(count):
        every = every * flag_ref[index]

    if unit == BLK:

        @pl.when(every != 0)
        def _():
            attend_rolled(held_ref[:, :HD], held_ref[:, HD:], q_ref, work_ref, score_ref)

    def body(index, carry):
        @pl.when(flag_ref[index] != 0)
        def _():
            rows = pl.ds(pl.multiple_of(index * unit, unit), unit)
            attend_block(False, None, held_ref[rows, :HD], held_ref[rows, HD:], q_ref, work_ref)

        return carry

    @pl.when(every == 0)
    def _():
        lax.fori_loop(0, count, body, 0)

    if split:
        own_out_ref[...] = work_ref[:, :QROWS]
        pair_out_ref[...] = work_ref[:, QROWS:]


def attend_more(flags, queries, state, arrays, split=False):
    unit, count = arrays[0].shape[0], len(arrays)
    half = jax.ShapeDtypeStruct((STATE, QROWS), jnp.float32)
    whole = jax.ShapeDtypeStruct((STATE, 2 * QROWS), jnp.float32)
    scratch = [
        pltpu.VMEM((count * unit, 2 * HD), jnp.bfloat16),
        pltpu.SemaphoreType.DMA((count,)),
        pltpu.VMEM((2, 3 * BLK if unit == BLK else 8, TILE), jnp.float32),
    ]
    if split:
        scratch.append(pltpu.VMEM((STATE, 2 * QROWS), jnp.float32))
    return pl.pallas_call(
        functools.partial(more_kernel, count, split),
        in_specs=[pl.BlockSpec(memory_space=pltpu.SMEM)]
        + [pl.BlockSpec(memory_space=pltpu.VMEM)] * 2
        + [pl.BlockSpec(memory_space=pl.ANY)] * count,
        out_shape=(half, half) if split else whole,
        scratch_shapes=scratch,
        compiler_params=params(),
        cost_estimate=cost(count * unit // BLK),
        name="more",
    )(flags, queries, state, *arrays)


def finish_kernel(own_ref, got_ref, out_ref, row_ref):
    scale = 1.4426950408889634 / HD**0.5
    for start in range(0, QROWS, TILE):
        cut = slice(start, start + TILE)
        first, second = own_ref[HD : HD + 1, cut], got_ref[HD : HD + 1, cut]
        best = jnp.maximum(first, second)
        first = jnp.exp2((first - best) * scale)
        second = jnp.exp2((second - best) * scale)
        total = own_ref[HD + 1 : HD + 2, cut] * first + got_ref[HD + 1 : HD + 2, cut] * second
        summed = own_ref[:HD, cut] * first + got_ref[:HD, cut] * second
        row_ref[cut, :] = jnp.transpose(summed / total)
    for head in range(GROUP):
        rows = row_ref[head * BLK : (head + 1) * BLK, :]
        out_ref[:, head * HD : (head + 1) * HD] = rows.astype(jnp.bfloat16)


def finish(own, got):
    return pl.pallas_call(
        finish_kernel,
        out_shape=jax.ShapeDtypeStruct((BLK, GROUP * HD), jnp.bfloat16),
        scratch_shapes=[pltpu.VMEM((QROWS, HD), jnp.float32)],
        compiler_params=params(),
        name="finish",
    )(own, got)


def page_kernel(place_ref, code_ref, *rest):
    count = (len(rest) - 4) // 2
    remote, own_ref, pair_ref = rest[:count], rest[count], rest[count + 1]
    held_ref, sems, arrays = rest[count + 2], rest[count + 3], rest[count + 4 :]
    copies = [
        pltpu.make_async_copy(remote[index], arrays[index], sems.at[index])
        for index in range(count)
    ]
    for copy in copies:
        copy.start()
    held_ref[...] = jnp.zeros_like(held_ref)
    y, z, core = place_ref[0], place_ref[1], place_ref[2]
    waited = set()
    for by_y in range(4):
        for by_z in range(4):
            if by_y == 0:
                index, base = by_z, 0
            else:
                index, base = 3 + by_y + (0, 3, 6, 3)[by_z], by_z // 3 * BLK
            if index not in waited:
                copies[index].wait()
                waited.add(index)
            array = arrays[index]
            source = (((y - by_y) & 3) * 4 + ((z - by_z) & 3)) * 2 + core
            for entry in range(2 * MOST):
                code = code_ref[source * 2 * MOST + entry]

                @pl.when(code >= 0)
                def _():
                    page = code >> 6
                    slot = (code & 63) + entry // MOST * PAGES
                    row = pl.multiple_of(base + (page >> 1) * 2 * PAGE, 2 * PAGE)
                    rows = array[pl.ds(row, 2 * PAGE), :].astype(jnp.float32)
                    rows = jnp.where((page & 1) == 1, rows[PAGE:], rows[:PAGE])
                    held_ref[pl.ds(pl.multiple_of(slot * PAGE, PAGE), PAGE), :] = rows

    own_ref[...] = held_ref[: PAGES * PAGE].astype(jnp.bfloat16)
    pair_ref[...] = held_ref[PAGES * PAGE :].astype(jnp.bfloat16)


def fetch_pages(place, codes, arrays):
    out = jax.ShapeDtypeStruct((PAGES * PAGE, 2 * HD), jnp.bfloat16)
    return pl.pallas_call(
        page_kernel,
        in_specs=[pl.BlockSpec(memory_space=pltpu.SMEM)] * 2
        + [pl.BlockSpec(memory_space=pl.ANY)] * len(arrays),
        out_shape=(out, out),
        scratch_shapes=[
            pltpu.VMEM((2 * PAGES * PAGE, 2 * HD), jnp.float32),
            pltpu.SemaphoreType.DMA((len(arrays),)),
        ]
        + [pltpu.VMEM(array.shape, array.dtype) for array in arrays],
        compiler_params=params(),
        name="pages",
    )(place, codes, *arrays)


def moves(step):
    pairs = []
    for y in range(4):
        for z in range(4):
            for core in range(2):
                to_y, to_z, to_core = step(y, z, core)
                pairs.append(((y * 4 + z) * 2 + core, (to_y * 4 + to_z) * 2 + to_core))
    return pairs


def along_y(value, count):
    return lax.ppermute(value, "seq", moves(lambda y, z, c: ((y + count) % 4, z, c)))


def along_z(value, count):
    return lax.ppermute(value, "seq", moves(lambda y, z, c: (y, (z + count) % 4, c)))


def other_core(value):
    return lax.ppermute(value, "seq", moves(lambda y, z, c: (y, z, 1 - c)))


def page_codes(targets, me):
    index = jnp.arange(PAGES, dtype=jnp.int32)
    codes = []
    for owner in (me, me ^ 1):
        slot = targets - owner * PAGES
        match = (slot >= 0) & (slot < PAGES)
        before = match[:, None, :] & (index[None, :] < index[:, None])
        rank = jnp.sum(before.astype(jnp.int32), axis=2)
        code = index * 64 + slot + 1
        for entry in range(MOST):
            codes.append(jnp.sum(jnp.where(match & (rank == entry), code, 0), axis=1) - 1)
    return jnp.stack(codes, axis=1).reshape(-1)


def held_here(targets, me):
    mine = me * PAGES + jnp.arange(PAGES, dtype=jnp.int32)
    same_core = (jnp.arange(SEQ, dtype=jnp.int32) % 2 == me % 2)[:, None]
    match = (targets[None] == mine[:, None, None]) & same_core[None]
    return jnp.any(match, axis=(1, 2))


def project(normed, weight):
    return jnp.dot(normed, weight, preferred_element_type=jnp.float32).astype(jnp.bfloat16)


def attention_and_pages(me, codes, keep, normed, weight):
    core, z, y = me % 2, (me // 2) % 4, me // 8
    kv = project(normed, weight[:, GROUP * HD :])
    normed, kv = lax.optimization_barrier((normed, kv))
    by_z = {0: kv, 1: along_z(kv, 1), 3: along_z(kv, 3)}
    none = {count: along_y(kv, count) for count in (1, 3, 2)}
    own_queries = project(normed, weight[:, : GROUP * HD])
    pair_queries = other_core(own_queries)

    def flag(*conditions):
        return jnp.stack([jnp.asarray(value, jnp.int32) for value in conditions])

    state, queries = attend_first(core, own_queries, pair_queries, kv)
    state, by_z[1], by_z[3] = lax.optimization_barrier((state, by_z[1], by_z[3]))
    kv, odd = lax.optimization_barrier((kv, jnp.concatenate([by_z[1], by_z[3]], axis=0)))
    by_z[2] = along_z(kv, 2)
    odd = {count: along_y(odd, count) for count in (1, 3, 2)}
    state = attend_more(
        flag(y >= 1, y >= 3, y >= 2), queries, state, [none[1], none[3], none[2]]
    )
    state, by_z[2] = lax.optimization_barrier((state, by_z[2]))
    two = {count: along_y(by_z[2], count) for count in (1, 3, 2)}
    state = attend_more(
        flag(z >= 1, z >= 3, z >= 2), queries, state, [by_z[1], by_z[3], by_z[2]]
    )
    state, odd[1], odd[3], odd[2] = lax.optimization_barrier((state, odd[1], odd[3], odd[2]))
    state = attend_more(flag(y >= 1, y >= 3, y >= 2), queries, state, [odd[1], odd[3], odd[2]])
    state, two[1], two[3], two[2] = lax.optimization_barrier((state, two[1], two[3], two[2]))
    own, sent = attend_more(
        flag(y >= 1, y >= 3, y >= 2), queries, state, [two[1], two[3], two[2]], split=True
    )
    got = other_core(sent)

    arrays = [by_z[count] for count in range(4)]
    arrays += [group[count] for group in (none, odd, two) for count in (1, 2, 3)]
    place = jnp.stack([y, z, core])
    own_pages, sent_pages = fetch_pages(place, codes, arrays)
    got_pages = other_core(sent_pages)
    attention = finish(own, got)
    attention, got_pages = lax.optimization_barrier((attention, got_pages))
    keep = keep.reshape(PAGES, 1, 1, 1)
    shape = (PAGES, PAGE, 2, HD)
    kv_cache = jnp.where(keep, own_pages.reshape(shape), got_pages.reshape(shape))
    return attention, kv_cache


def on_device(
    features,
    conv_weight,
    conv_bias,
    embed_weight,
    position_table,
    norm_gain,
    qkv_weight,
    page_owner,
    page_slot,
):
    me = lax.axis_index("seq").astype(jnp.int32)
    tensor = lax.axis_index("tensor").astype(jnp.int32)
    tensor_count = lax.axis_size("tensor")
    weight = lax.all_gather(qkv_weight, "seq", axis=0, tiled=True)
    parts = partial_latents(features, conv_weight)
    own = parts[: FRAMES * EXT].reshape(FRAMES, EXT * LAT)
    target = (page_owner * PAGES + page_slot).astype(jnp.float32)
    target = jnp.broadcast_to(target, (FRAMES, PAGES))
    message = jnp.concatenate([own, target], axis=1)
    message = jnp.pad(message, ((0, 0), (0, 512 - message.shape[1])))
    message = jnp.broadcast_to(message[:, None], (FRAMES, SEQ // FRAMES, 512)).reshape(SEQ, 512)
    message = lax.all_to_all(message, "seq", split_axis=0, concat_axis=0, tiled=True)
    gain = norm_gain.reshape(1, -1)
    message, gain = lax.optimization_barrier((message, gain))
    targets = message[:, EXT * LAT : EXT * LAT + PAGES].astype(jnp.int32)
    offset = tensor - me % (SEQ // FRAMES)
    latent = place_latents(message[:, : EXT * LAT].reshape(SEQ * EXT, LAT), offset)
    for bit in (1, 2, 4):
        swap = [(i, i ^ bit) for i in range(tensor_count)]
        latent = latent + lax.ppermute(latent, "tensor", swap)
    latent = latent + conv_bias[:, None]
    normed = normed_hidden(latent, embed_weight, position_table, gain)
    codes, keep = page_codes(targets, me), held_here(targets, me)
    normed, codes, keep = lax.optimization_barrier((normed, codes, keep))
    return attention_and_pages(me, codes, keep, normed, weight)


def solution(mesh):
    placed = (
        P(None, "tensor", "seq", None),
        P(),
        P(),
        P(),
        P("seq", None),
        P(),
        P("seq", "tensor"),
        P("seq"),
        P("seq"),
    )
    return jax.shard_map(
        on_device,
        mesh=mesh,
        in_specs=placed,
        out_specs=(P("seq", "tensor"), P("seq", None, None, "tensor")),
        check_vma=False,
    )
```

profile of v0, /device:TPU:25, one launch (start us, length us, event | category | flops | bytes accessed | tf_op | source)
XLA Modules:
  0.0 148.2 jit_solution(1858937242476307582)
XLA Ops:
  7.2 0.0 all-gather.2.cloned.1.call-start
  7.2 0.7 all-gather.2.cloned.1.call-update
  7.9 1.0 copy-done.1
  8.9 0.8 copy-done.3
  9.7 0.5 conv.1
  10.2 0.1 reshape.129
  10.3 0.7 add_convert_fusion.2
  11.0 0.1 pad.14.clone
  11.1 0.7 all_to_all.8
  11.8 9.3 %all-to-all-start = ((f32[32,1,512]{2,1,0:T(1,128)}), f32[32,1,512]{2,1,0:T(1,128)S(1)}, u32[]{:S(2)}, u32[]{:S(2)}) async-start(f32[32,1,512]{2,1,0:T(1,128)} %all_to_all.8), calls=%async_computation | async-start | bytes 131072 | tf_op jit(solution)/shard_map/all_to_all | solution.py:571
  21.1 0.7 reshape.130.gain_ref
  21.9 4.9 %all-to-all-done = f32[32,1,512]{2,1,0:T(1,128)S(1)} async-done(((f32[32,1,512]{2,1,0:T(1,128)}), f32[32,1,512]{2,1,0:T(1,128)S(1)}, u32[]{:S(2)}, u32[]{:S(2)}) %all-to-all-start) | async-done | bytes 65568 | tf_op jit(solution)/shard_map/all_to_all | solution.py:571
  26.8 0.2 reshape.131.parts_ref
  26.9 0.7 copy-done.4
  27.6 0.7 place.1
  28.3 4.2 %collective-permute-start = (f32[16,384]{1,0:T(8,128)S(1)}, f32[16,384]{1,0:T(8,128)S(1)}, u32[]{:S(2)}, u32[]{:S(2)}) collective-permute-start(f32[16,384]{1,0:T(8,128)S(1)} %place.1), channel_id=1, source_target_pairs={{0,1},{1,0},{2,3},{3,2},{4,5},{5,4},{6,7},{7,6},{8,9},{9,8},{10,11... | collective-permute-start | bytes 73736 | tf_op jit(solution)/shard_map/ppermute | solution.py:579
  32.5 0.1 compare_and_fusion.1
  32.6 1.2 convert_reduce_fusion
  33.8 0.3 select_reduce_fusion
  34.0 0.1 slice_convert_fusion
  34.1 1.2 collective-permute-done
  35.3 1.2 collective-permute-start.1
  36.5 1.9 %collective-permute-done.1 = f32[16,384]{1,0:T(8,128)S(1)} collective-permute-done((f32[16,384]{1,0:T(8,128)S(1)}, f32[16,384]{1,0:T(8,128)S(1)}, u32[]{:S(2)}, u32[]{:S(2)}) %collective-permute-start.1) | collective-permute-done | bytes 24608 | tf_op jit(solution)/shard_map/ppermute | solution.py:579
  38.4 2.8 %collective-permute-start.2 = (f32[16,384]{1,0:T(8,128)S(1)}, f32[16,384]{1,0:T(8,128)S(1)}, u32[]{:S(2)}, u32[]{:S(2)}) collective-permute-start(f32[16,384]{1,0:T(8,128)S(1)} %add.135), channel_id=1, source_target_pairs={{0,4},{1,5},{2,6},{3,7},{4,0},{5,1},{6,2},{7,3},{8,12},{9,13},{10,... | collective-permute-start | bytes 73736 | tf_op jit(solution)/shard_map/ppermute | solution.py:579
  41.1 1.0 and_reduce_fusion
  42.2 0.1 copy.20
  42.3 0.1 reshape.132.code_ref
  42.4 0.4 collective-permute-done.2
  42.7 0.7 add_add_fusion.latent_ref
  43.5 2.0 %copy-done = bf16[320,5120]{1,0:T(8,128)(2,1)S(1)} copy-done((bf16[320,5120]{1,0:T(8,128)(2,1)S(1)}, bf16[320,5120]{1,0:T(8,128)(2,1)}, u32[]{:S(2)}) %copy-start) | copy-done | bytes 3276824
  45.5 0.9 copy-done.2
  46.4 4.2 %hidden.1 = bf16[320,5120]{1,0:T(8,128)(2,1)S(1)} custom-call(f32[16,384]{1,0:T(8,128)S(1)} %add_add_fusion.latent_ref, bf16[16,5120]{1,0:T(8,128)(2,1)S(1)} %copy-done.2, bf16[320,5120]{1,0:T(8,128)(2,1)S(1)} %copy-done, bf16[1,5120]{1,0:T(2,128)(2,1)S(1)} %reshape.130.gain_ref), custom_call_target="tpu_custom_call" | custom-call | tf_op jit(solution)/shard_map/hidden/pallas_call | solution.py:164
  50.6 30.2 %all-gather.2.cloned.1.call-done = bf16[5120,768]{1,0:T(8,128)(2,1)} async-done(((bf16[160,768]{1,0:T(8,128)(2,1)}), bf16[5120,768]{1,0:T(8,128)(2,1)}) %all-gather.2.cloned.1.call-update) | async-done | bytes 7864336 | tf_op jit(solution)/shard_map/all_gather | solution.py:563
  80.8 2.9 %fusion.7.kv_ref.rest_0_ = bf16[320,256]{1,0:T(8,128)(2,1)S(1)} fusion(bf16[320,5120]{1,0:T(8,128)(2,1)S(1)} %hidden.1, bf16[5120,768]{1,0:T(8,128)(2,1)} %all-gather.2.cloned.1.call-done), kind=kOutput, calls=%fused_computation.5 | convolution fusion | flops 838942720 | bytes 6062080 | tf_op jit(solution)/shard_map/dot_general | solution.py:500
  83.7 1.1 copy-done.5
  84.8 2.6 %fusion.4.own_ref = bf16[320,512]{1,0:T(8,128)(2,1)} fusion(bf16[320,5120]{1,0:T(8,128)(2,1)S(1)} %hidden.1, bf16[5120,768]{1,0:T(8,128)(2,1)S(1)} %copy-done.5), kind=kOutput, calls=%fused_computation.4 | convolution fusion | flops 1677885440 | bytes 8847360 | tf_op jit(solution)/shard_map/dot_general | solution.py:500
  87.4 0.3 collective-permute-start.3
  87.7 2.4 %collective-permute-start.5 = (bf16[320,256]{1,0:T(8,128)(2,1)S(1)}, bf16[320,256]{1,0:T(8,128)(2,1)S(1)}, u32[]{:S(2)}, u32[]{:S(2)}) collective-permute-start(bf16[320,256]{1,0:T(8,128)(2,1)S(1)} %fusion.7.kv_ref.rest_0_), channel_id=1, source_target_pairs={{0,48},{8,56},{16,0},{24,8},{32,16},{40,24},{48,32},{56,40},{64,11... | collective-permute-start | bytes 491528 | tf_op jit(solution)/shard_map/ppermute | solution.py:471
  90.1 1.3 collective-permute-start.8
  91.4 0.5 collective-permute-start.7
  91.9 0.1 add_convert_fusion.flag_ref
  92.0 2.3 %collective-permute-start.6 = (bf16[320,256]{1,0:T(8,128)(2,1)S(1)}, bf16[320,256]{1,0:T(8,128)(2,1)S(1)}, u32[]{:S(2)}, u32[]{:S(2)}) collective-permute-start(bf16[320,256]{1,0:T(8,128)(2,1)S(1)} %fusion.7.kv_ref.rest_0_), channel_id=1, source_target_pairs={{0,64},{8,72},{16,80},{24,88},{32,96},{40,104},{48,112},{56,120},{... | collective-permute-start | bytes 491528 | tf_op jit(solution)/shard_map/ppermute | solution.py:467
  94.2 3.0 %first.1 = (f32[136,2560]{1,0:T(8,128)S(1)}, bf16[2560,128]{1,0:T(8,128)(2,1)S(1)}) custom-call(s32[1]{0:T(128)} %bitcast.3.core_ref, bf16[320,512]{1,0:T(8,128)(2,1)} %fusion.4.own_ref, bf16[320,512]{1,0:T(8,128)(2,1)S(1)} %collective-permute-done.3.pair_ref, bf16[320,256]{1,0:T(8,128)(2,1)S(1)} %fusion.7.kv_ref.rest_0_), custom_call_target="tpu_custom_call" | custom-call | flops 419430400 | bytes 3145728 | tf_op jit(solution)/shard_map/first/pallas_call | solution.py:292
  97.2 0.5 collective-permute-done.4.rest_0_.rest_1_
  97.8 1.9 %collective-permute-start.12 = (bf16[640,256]{1,0:T(8,128)(2,1)S(1)}, bf16[640,256]{1,0:T(8,128)(2,1)S(1)}, u32[]{:S(2)}, u32[]{:S(2)}) collective-permute-start(bf16[640,256]{1,0:T(8,128)(2,1)S(1)} %pad_maximum_fusion), channel_id=1, source_target_pairs={{0,128},{8,136},{16,144},{24,152},{32,160},{40,168},{48,176},{56,1... | collective-permute-start | bytes 983048 | tf_op jit(solution)/shard_map/ppermute | solution.py:467
  99.6 0.9 collective-permute-start.11
  100.5 1.8 %collective-permute-start.10 = (bf16[640,256]{1,0:T(8,128)(2,1)S(1)}, bf16[640,256]{1,0:T(8,128)(2,1)S(1)}, u32[]{:S(2)}, u32[]{:S(2)}) collective-permute-start(bf16[640,256]{1,0:T(8,128)(2,1)S(1)} %pad_maximum_fusion), channel_id=1, source_target_pairs={{0,64},{8,72},{16,80},{24,88},{32,96},{40,104},{48,112},{56,120},{... | collective-permute-start | bytes 983048 | tf_op jit(solution)/shard_map/ppermute | solution.py:467
  102.3 2.3 %collective-permute-start.9 = (bf16[320,256]{1,0:T(8,128)(2,1)S(1)}, bf16[320,256]{1,0:T(8,128)(2,1)S(1)}, u32[]{:S(2)}, u32[]{:S(2)}) collective-permute-start(bf16[320,256]{1,0:T(8,128)(2,1)S(1)} %fusion.7.kv_ref.rest_0_), channel_id=1, source_target_pairs={{0,32},{8,40},{16,48},{24,56},{32,0},{40,8},{48,16},{56,24},{64,96... | collective-permute-start | bytes 491528 | tf_op jit(solution)/shard_map/ppermute | solution.py:471
  104.6 0.1 add_convert_fusion.1.flag_ref
  104.7 5.7 %more.4.state_ref = f32[136,2560]{1,0:T(8,128)S(1)} custom-call(s32[3]{0:T(128)S(1)} %add_convert_fusion.flag_ref, bf16[2560,128]{1,0:T(8,128)(2,1)S(1)} %get-tuple-element.37.q_ref, f32[136,2560]{1,0:T(8,128)S(1)} %get-tuple-element.39.state_ref, bf16[320,256]{1,0:T(8,128)(2,1)S(1)} %collective-permute-done.6.rest_0_.rest_4_, ...), custom_call_target="tpu_custom_call" | custom-call | flops 1258291200 | bytes 3145728 | tf_op jit(solution)/shard_map/more/pallas_call | solution.py:360
  110.4 1.6 %collective-permute-done.9.rest_2_ = bf16[320,256]{1,0:T(8,128)(2,1)S(1)} collective-permute-done((bf16[320,256]{1,0:T(8,128)(2,1)S(1)}, bf16[320,256]{1,0:T(8,128)(2,1)S(1)}, u32[]{:S(2)}, u32[]{:S(2)}) %collective-permute-start.9) | collective-permute-done | bytes 163872 | tf_op jit(solution)/shard_map/ppermute | solution.py:471
  112.0 0.6 collective-permute-start.15
  112.7 1.3 collective-permute-start.14
  114.0 1.3 more.5.state_ref
  115.4 1.6 %collective-permute-start.13 = (bf16[320,256]{1,0:T(8,128)(2,1)S(1)}, bf16[320,256]{1,0:T(8,128)(2,1)S(1)}, u32[]{:S(2)}, u32[]{:S(2)}) collective-permute-start(bf16[320,256]{1,0:T(8,128)(2,1)S(1)} %collective-permute-done.9.rest_2_), channel_id=1, source_target_pairs={{0,64},{8,72},{16,80},{24,88},{32,96},{40,104},{48,112},{56,120},{... | collective-permute-start | bytes 491528 | tf_op jit(solution)/shard_map/ppermute | solution.py:467
  117.0 9.6 %more.6.state_ref = f32[136,2560]{1,0:T(8,128)S(1)} custom-call(s32[3]{0:T(128)S(1)} %add_convert_fusion.flag_ref, bf16[2560,128]{1,0:T(8,128)(2,1)S(1)} %get-tuple-element.37.q_ref, f32[136,2560]{1,0:T(8,128)S(1)} %more.5.state_ref, bf16[640,256]{1,0:T(8,128)(2,1)S(1)} %collective-permute-done.10.rest_0_.rest_7_, ...), custom_call_target="tpu_custom_call" | custom-call | flops 2516582400 | bytes 3145728 | tf_op jit(solution)/shard_map/more/pallas_call | solution.py:360
  126.6 5.8 %more.7 = (f32[136,1280]{1,0:T(8,128)S(1)}, f32[136,1280]{1,0:T(8,128)S(1)}) custom-call(s32[3]{0:T(128)S(1)} %add_convert_fusion.flag_ref, bf16[2560,128]{1,0:T(8,128)(2,1)S(1)} %get-tuple-element.37.q_ref, f32[136,2560]{1,0:T(8,128)S(1)} %more.6.state_ref, bf16[320,256]{1,0:T(8,128)(2,1)S(1)} %collective-permute-done.13.rest_0_.rest_10_, ...), custom_call_target="tpu_custom_call" | custom-call | flops 1258291200 | bytes 3145728 | tf_op jit(solution)/shard_map/more/pallas_call | solution.py:360
  132.4 2.3 %collective-permute-start.16 = (f32[136,1280]{1,0:T(8,128)S(1)}, f32[136,1280]{1,0:T(8,128)S(1)}, u32[]{:S(2)}, u32[]{:S(2)}) collective-permute-start(f32[136,1280]{1,0:T(8,128)S(1)} %get-tuple-element.55), channel_id=1, source_target_pairs={{0,8},{8,0},{16,24},{24,16},{32,40},{40,32},{48,56},{56,48},{64,72... | collective-permute-start | bytes 2088968 | tf_op jit(solution)/shard_map/ppermute | solution.py:475
  134.7 0.1 pad_add_fusion.place_ref
  134.8 4.1 %pages.1 = (bf16[320,256]{1,0:T(8,128)(2,1)S(1)}, bf16[320,256]{1,0:T(8,128)(2,1)S(1)}) custom-call(s32[3]{0:T(128)S(1)} %pad_add_fusion.place_ref, s32[192]{0:T(256)S(1)} %reshape.132.code_ref, bf16[320,256]{1,0:T(8,128)(2,1)S(1)} %fusion.7.kv_ref.rest_0_, bf16[320,256]{1,0:T(8,128)(2,1)S(1)} %collective-permute-done.4.rest_0_.rest_1_, ...), custom_call_target="tpu_custom_call" | custom-call | tf_op jit(solution)/shard_map/pages/pallas_call | solution.py:441
  138.9 0.1 collective-permute-start.17
  139.0 1.0 finish.1
  140.0 0.4 collective-permute-done.17
  140.4 0.9 broadcast_select_fusion
  (35 shorter events, 0.2 us)
Async XLA Ops:
  7.2 73.6 %all-gather.2.cloned.1.call-start = ((), (), s32[]{:S(2)}) async-start(), calls=%async_computation.1 | async-start | bytes 8110080 | tf_op jit(solution)/shard_map/all_gather | solution.py:563
  7.9 1.0 copy-start.1
  8.9 0.8 copy-start.3
  11.8 14.9 %all-to-all-start = ((f32[32,1,512]{2,1,0:T(1,128)}), f32[32,1,512]{2,1,0:T(1,128)S(1)}, u32[]{:S(2)}, u32[]{:S(2)}) async-start(f32[32,1,512]{2,1,0:T(1,128)} %all_to_all.8), calls=%async_computation | async-start | bytes 131072 | tf_op jit(solution)/shard_map/all_to_all | solution.py:571
  26.9 0.7 copy-start.4
  28.3 7.0 %collective-permute-start = (f32[16,384]{1,0:T(8,128)S(1)}, f32[16,384]{1,0:T(8,128)S(1)}, u32[]{:S(2)}, u32[]{:S(2)}) collective-permute-start(f32[16,384]{1,0:T(8,128)S(1)} %place.1), channel_id=1, source_target_pairs={{0,1},{1,0},{2,3},{3,2},{4,5},{5,4},{6,7},{7,6},{8,9},{9,8},{10,11... | collective-permute-start | bytes 73736 | tf_op jit(solution)/shard_map/ppermute | solution.py:579
  35.3 3.1 %collective-permute-start.1 = (f32[16,384]{1,0:T(8,128)S(1)}, f32[16,384]{1,0:T(8,128)S(1)}, u32[]{:S(2)}, u32[]{:S(2)}) collective-permute-start(f32[16,384]{1,0:T(8,128)S(1)} %add.134), channel_id=1, source_target_pairs={{0,2},{1,3},{2,0},{3,1},{4,6},{5,7},{6,4},{7,5},{8,10},{9,11},{10,... | collective-permute-start | bytes 73736 | tf_op jit(solution)/shard_map/ppermute | solution.py:579
  38.4 4.4 %collective-permute-start.2 = (f32[16,384]{1,0:T(8,128)S(1)}, f32[16,384]{1,0:T(8,128)S(1)}, u32[]{:S(2)}, u32[]{:S(2)}) collective-permute-start(f32[16,384]{1,0:T(8,128)S(1)} %add.135), channel_id=1, source_target_pairs={{0,4},{1,5},{2,6},{3,7},{4,0},{5,1},{6,2},{7,3},{8,12},{9,13},{10,... | collective-permute-start | bytes 73736 | tf_op jit(solution)/shard_map/ppermute | solution.py:579
  43.5 2.0 %copy-start = (bf16[320,5120]{1,0:T(8,128)(2,1)S(1)}, bf16[320,5120]{1,0:T(8,128)(2,1)}, u32[]{:S(2)}) copy-start(bf16[320,5120]{1,0:T(8,128)(2,1)} %table_ref.1) | copy-start | bytes 9830404
  45.5 0.9 copy-start.2
  80.8 4.0 %copy-start.5 = (bf16[5120,768]{1,0:T(8,128)(2,1)S(1)}, bf16[5120,768]{1,0:T(8,128)(2,1)}, u32[]{:S(2)}) copy-start(bf16[5120,768]{1,0:T(8,128)(2,1)} %all-gather.2.cloned.1.call-done) | copy-start | bytes 23592964
  87.4 4.5 %collective-permute-start.3 = (bf16[320,512]{1,0:T(8,128)(2,1)}, bf16[320,512]{1,0:T(8,128)(2,1)S(1)}, u32[]{:S(2)}, u32[]{:S(2)}) collective-permute-start(bf16[320,512]{1,0:T(8,128)(2,1)} %fusion.4.own_ref), channel_id=1, source_target_pairs={{0,8},{8,0},{16,24},{24,16},{32,40},{40,32},{48,56},{56,48},{64,72... | collective-permute-start | bytes 983048 | tf_op jit(solution)/shard_map/ppermute | solution.py:475
  87.7 9.5 %collective-permute-start.5 = (bf16[320,256]{1,0:T(8,128)(2,1)S(1)}, bf16[320,256]{1,0:T(8,128)(2,1)S(1)}, u32[]{:S(2)}, u32[]{:S(2)}) collective-permute-start(bf16[320,256]{1,0:T(8,128)(2,1)S(1)} %fusion.7.kv_ref.rest_0_), channel_id=1, source_target_pairs={{0,48},{8,56},{16,0},{24,8},{32,16},{40,24},{48,32},{56,40},{64,11... | collective-permute-start | bytes 491528 | tf_op jit(solution)/shard_map/ppermute | solution.py:471
  90.1 7.6 %collective-permute-start.4 = (bf16[320,256]{1,0:T(8,128)(2,1)S(1)}, bf16[320,256]{1,0:T(8,128)(2,1)S(1)}, u32[]{:S(2)}, u32[]{:S(2)}) collective-permute-start(bf16[320,256]{1,0:T(8,128)(2,1)S(1)} %fusion.7.kv_ref.rest_0_), channel_id=1, source_target_pairs={{0,16},{8,24},{16,32},{24,40},{32,48},{40,56},{48,0},{56,8},{64,80... | collective-permute-start | bytes 491528 | tf_op jit(solution)/shard_map/ppermute | solution.py:471
  90.1 10.4 %collective-permute-start.8 = (bf16[320,256]{1,0:T(8,128)(2,1)S(1)}, bf16[320,256]{1,0:T(8,128)(2,1)S(1)}, u32[]{:S(2)}, u32[]{:S(2)}) collective-permute-start(bf16[320,256]{1,0:T(8,128)(2,1)S(1)} %fusion.7.kv_ref.rest_0_), channel_id=1, source_target_pairs={{0,128},{8,136},{16,144},{24,152},{32,160},{40,168},{48,176},{56,1... | collective-permute-start | bytes 491528 | tf_op jit(solution)/shard_map/ppermute | solution.py:467
  91.4 10.9 %collective-permute-start.7 = (bf16[320,256]{1,0:T(8,128)(2,1)S(1)}, bf16[320,256]{1,0:T(8,128)(2,1)S(1)}, u32[]{:S(2)}, u32[]{:S(2)}) collective-permute-start(bf16[320,256]{1,0:T(8,128)(2,1)S(1)} %fusion.7.kv_ref.rest_0_), channel_id=1, source_target_pairs={{0,192},{8,200},{16,208},{24,216},{32,224},{40,232},{48,240},{56,2... | collective-permute-start | bytes 491528 | tf_op jit(solution)/shard_map/ppermute | solution.py:467
  92.0 12.7 %collective-permute-start.6 = (bf16[320,256]{1,0:T(8,128)(2,1)S(1)}, bf16[320,256]{1,0:T(8,128)(2,1)S(1)}, u32[]{:S(2)}, u32[]{:S(2)}) collective-permute-start(bf16[320,256]{1,0:T(8,128)(2,1)S(1)} %fusion.7.kv_ref.rest_0_), channel_id=1, source_target_pairs={{0,64},{8,72},{16,80},{24,88},{32,96},{40,104},{48,112},{56,120},{... | collective-permute-start | bytes 491528 | tf_op jit(solution)/shard_map/ppermute | solution.py:467
  97.8 17.6 %collective-permute-start.12 = (bf16[640,256]{1,0:T(8,128)(2,1)S(1)}, bf16[640,256]{1,0:T(8,128)(2,1)S(1)}, u32[]{:S(2)}, u32[]{:S(2)}) collective-permute-start(bf16[640,256]{1,0:T(8,128)(2,1)S(1)} %pad_maximum_fusion), channel_id=1, source_target_pairs={{0,128},{8,136},{16,144},{24,152},{32,160},{40,168},{48,176},{56,1... | collective-permute-start | bytes 983048 | tf_op jit(solution)/shard_map/ppermute | solution.py:467
  99.6 17.4 %collective-permute-start.11 = (bf16[640,256]{1,0:T(8,128)(2,1)S(1)}, bf16[640,256]{1,0:T(8,128)(2,1)S(1)}, u32[]{:S(2)}, u32[]{:S(2)}) collective-permute-start(bf16[640,256]{1,0:T(8,128)(2,1)S(1)} %pad_maximum_fusion), channel_id=1, source_target_pairs={{0,192},{8,200},{16,208},{24,216},{32,224},{40,232},{48,240},{56,2... | collective-permute-start | bytes 983048 | tf_op jit(solution)/shard_map/ppermute | solution.py:467
  100.5 16.5 %collective-permute-start.10 = (bf16[640,256]{1,0:T(8,128)(2,1)S(1)}, bf16[640,256]{1,0:T(8,128)(2,1)S(1)}, u32[]{:S(2)}, u32[]{:S(2)}) collective-permute-start(bf16[640,256]{1,0:T(8,128)(2,1)S(1)} %pad_maximum_fusion), channel_id=1, source_target_pairs={{0,64},{8,72},{16,80},{24,88},{32,96},{40,104},{48,112},{56,120},{... | collective-permute-start | bytes 983048 | tf_op jit(solution)/shard_map/ppermute | solution.py:467
  102.3 9.7 %collective-permute-start.9 = (bf16[320,256]{1,0:T(8,128)(2,1)S(1)}, bf16[320,256]{1,0:T(8,128)(2,1)S(1)}, u32[]{:S(2)}, u32[]{:S(2)}) collective-permute-start(bf16[320,256]{1,0:T(8,128)(2,1)S(1)} %fusion.7.kv_ref.rest_0_), channel_id=1, source_target_pairs={{0,32},{8,40},{16,48},{24,56},{32,0},{40,8},{48,16},{56,24},{64,96... | collective-permute-start | bytes 491528 | tf_op jit(solution)/shard_map/ppermute | solution.py:471
  112.0 14.6 %collective-permute-start.15 = (bf16[320,256]{1,0:T(8,128)(2,1)S(1)}, bf16[320,256]{1,0:T(8,128)(2,1)S(1)}, u32[]{:S(2)}, u32[]{:S(2)}) collective-permute-start(bf16[320,256]{1,0:T(8,128)(2,1)S(1)} %collective-permute-done.9.rest_2_), channel_id=1, source_target_pairs={{0,128},{8,136},{16,144},{24,152},{32,160},{40,168},{48,176},{56,1... | collective-permute-start | bytes 491528 | tf_op jit(solution)/shard_map/ppermute | solution.py:467
  112.7 13.9 %collective-permute-start.14 = (bf16[320,256]{1,0:T(8,128)(2,1)S(1)}, bf16[320,256]{1,0:T(8,128)(2,1)S(1)}, u32[]{:S(2)}, u32[]{:S(2)}) collective-permute-start(bf16[320,256]{1,0:T(8,128)(2,1)S(1)} %collective-permute-done.9.rest_2_), channel_id=1, source_target_pairs={{0,192},{8,200},{16,208},{24,216},{32,224},{40,232},{48,240},{56,2... | collective-permute-start | bytes 491528 | tf_op jit(solution)/shard_map/ppermute | solution.py:467
  115.4 11.3 %collective-permute-start.13 = (bf16[320,256]{1,0:T(8,128)(2,1)S(1)}, bf16[320,256]{1,0:T(8,128)(2,1)S(1)}, u32[]{:S(2)}, u32[]{:S(2)}) collective-permute-start(bf16[320,256]{1,0:T(8,128)(2,1)S(1)} %collective-permute-done.9.rest_2_), channel_id=1, source_target_pairs={{0,64},{8,72},{16,80},{24,88},{32,96},{40,104},{48,112},{56,120},{... | collective-permute-start | bytes 491528 | tf_op jit(solution)/shard_map/ppermute | solution.py:467
  132.4 6.6 %collective-permute-start.16 = (f32[136,1280]{1,0:T(8,128)S(1)}, f32[136,1280]{1,0:T(8,128)S(1)}, u32[]{:S(2)}, u32[]{:S(2)}) collective-permute-start(f32[136,1280]{1,0:T(8,128)S(1)} %get-tuple-element.55), channel_id=1, source_target_pairs={{0,8},{8,0},{16,24},{24,16},{32,40},{40,32},{48,56},{56,48},{64,72... | collective-permute-start | bytes 2088968 | tf_op jit(solution)/shard_map/ppermute | solution.py:475
  138.9 1.5 %collective-permute-start.17 = (bf16[320,256]{1,0:T(8,128)(2,1)S(1)}, bf16[320,256]{1,0:T(8,128)(2,1)S(1)}, u32[]{:S(2)}, u32[]{:S(2)}) collective-permute-start(bf16[320,256]{1,0:T(8,128)(2,1)S(1)} %get-tuple-element.57), channel_id=1, source_target_pairs={{0,8},{8,0},{16,24},{24,16},{32,40},{40,32},{48,56},{56,48},{64,72... | collective-permute-start | bytes 491528 | tf_op jit(solution)/shard_map/ppermute | solution.py:475
Sparse Core Ops, SparseCore 0:
  9.9 70.8 all-gather.1
where the time goes:
time: 151 us; the launch traced here: 148 us
  waiting for transfers between devices  41.7 us (28%)
  starting transfers between devices  37 us (25%)
  Pallas kernels  35.9 us (24%)
  between operations  14.3 us (9%)
  local copies, waits for them, and re-layouts  8.44 us (6%)
  matrix products  5.57 us (4%)
  other arithmetic  5.22 us (3%)
    all_gather x1, waiting for transfers between devices, on_device(): weight = lax.all_gather(qkv_weight, 'seq', axis=0, tiled=True)  30.2 us
    pallas_call x4, Pallas kernels, attend_more(): pl.pallas_call(functools.partial(more_kernel, count, split), in_specs=[pl...  22.5 us
    ppermute x9, starting transfers between devices, along_y(): lax.ppermute(value, 'seq', moves(lambda y, z, c: ((y + count) % 4, z, c)))  12.1 us
    all_to_all x1, starting transfers between devices, on_device(): lax.all_to_all(message, 'seq', split_axis=0, concat_axis=0, tiled=True)  9.26 us
    ppermute x3, starting transfers between devices, on_device(): latent = latent + lax.ppermute(latent, 'tensor', swap)  8.17 us
    unnamed x13, local copies, waits for them, and re-layouts  6.46 us
    dot_general x2, matrix products, project(): jnp.dot(normed, weight, preferred_element_type=jnp.float32)  5.57 us
    all_to_all x1, waiting for transfers between devices, on_device(): lax.all_to_all(message, 'seq', split_axis=0, concat_axis=0, tiled=True)  4.85 us
  transfers between devices with their start and end apart: 20, of which 8 were waited for; matrix products, arithmetic and copies ran while one was open for 4% of the time, Pallas kernels for 20%

commit v1 on v0

--- a/solution.py
+++ b/solution.py
@@ -506,6 +506,7 @@
     normed, kv = lax.optimization_barrier((normed, kv))
     by_z = {0: kv, 1: along_z(kv, 1), 3: along_z(kv, 3)}
     none = {count: along_y(kv, count) for count in (1, 3, 2)}
+    by_z[1], by_z[3], normed = lax.optimization_barrier((by_z[1], by_z[3], normed))
     own_queries = project(normed, weight[:, : GROUP * HD])
     pair_queries = other_core(own_queries)
 
@@ -513,7 +514,6 @@
         return jnp.stack([jnp.asarray(value, jnp.int32) for value in conditions])
 
     state, queries = attend_first(core, own_queries, pair_queries, kv)
-    state, by_z[1], by_z[3] = lax.optimization_barrier((state, by_z[1], by_z[3]))
     kv, odd = lax.optimization_barrier((kv, jnp.concatenate([by_z[1], by_z[3]], axis=0)))
     by_z[2] = along_z(kv, 2)
     odd = {count: along_y(odd, count) for count in (1, 3, 2)}

time: 151 us -> 159 us (1.053)
  waiting for transfers between devices: 41.7 us -> 49.8 us
    ppermute x3, waiting for transfers between devices: 2.12 us -> 7.69 us  [along_z(): lax.ppermute(value, 'seq', moves(lambda y, z, c: (y, (z + count) % 4, c)))]
    ppermute x9, starting transfers between devices: 12.1 us -> 7.61 us  [along_y(): lax.ppermute(value, 'seq', moves(lambda y, z, c: ((y + count) % 4, z, c)))]
    ppermute x3, starting transfers between devices: 4.7 us -> 7.39 us  [along_z(): lax.ppermute(value, 'seq', moves(lambda y, z, c: (y, (z + count) % 4, c)))]
    ppermute x9, waiting for transfers between devices: 0.02 us -> 2.56 us  [along_y(): lax.ppermute(value, 'seq', moves(lambda y, z, c: ((y + count) % 4, z, c)))]
    ppermute x3, starting transfers between devices: 2.66 us -> 4.34 us  [other_core(): return lax.ppermute(value, 'seq', moves(lambda y, z, c: (y, z, 1 - c)))]
    unnamed x13 -> x19, local copies, waits for them, and re-layouts: 6.46 us -> 6.31 us
  transfers between devices with their start and end apart: 20 -> 20, of which waited for: 8 -> 10; matrix products, arithmetic and copies ran while one was open for 4% -> 4% of each run, Pallas kernels for 20% -> 19%
where the time goes in v1:
time: 159 us; the launch traced here: 157 us
  waiting for transfers between devices  49.8 us (31%)
  starting transfers between devices  36.8 us (23%)
  Pallas kernels  36 us (23%)
  between operations  14.3 us (9%)
  local copies, waits for them, and re-layouts  8.29 us (5%)
  other arithmetic  6.14 us (4%)
  matrix products  5.57 us (4%)
    all_gather x1, waiting for transfers between devices, on_device(): weight = lax.all_gather(qkv_weight, 'seq', axis=0, tiled=True)  30.2 us
    pallas_call x4, Pallas kernels, attend_more(): pl.pallas_call(functools.partial(more_kernel, count, split), in_specs=[pl...  22.7 us
    all_to_all x1, starting transfers between devices, on_device(): lax.all_to_all(message, 'seq', split_axis=0, concat_axis=0, tiled=True)  9.26 us
    ppermute x3, starting transfers between devices, on_device(): latent = latent + lax.ppermute(latent, 'tensor', swap)  8.17 us
    ppermute x3, waiting for transfers between devices, along_z(): lax.ppermute(value, 'seq', moves(lambda y, z, c: (y, (z + count) % 4, c)))  7.69 us
    ppermute x9, starting transfers between devices, along_y(): lax.ppermute(value, 'seq', moves(lambda y, z, c: ((y + count) % 4, z, c)))  7.61 us
    ppermute x3, starting transfers between devices, along_z(): lax.ppermute(value, 'seq', moves(lambda y, z, c: (y, (z + count) % 4, c)))  7.39 us
    unnamed x19, local copies, waits for them, and re-layouts  6.31 us
  transfers between devices with their start and end apart: 20, of which 10 were waited for; matrix products, arithmetic and copies ran while one was open for 4% of the time, Pallas kernels for 19%

profile of v1, /device:TPU:25, one launch (start us, length us, event | category | flops | bytes accessed | tf_op | source)
XLA Modules:
  0.0 157.0 jit_solution(5082867528748196117)
XLA Ops:
  7.2 0.7 all-gather.2.cloned.1.call-update
  7.9 1.0 copy-done.1
  8.9 0.8 copy-done.6
  9.7 0.5 conv.1
  10.2 0.1 reshape.129
  10.3 0.7 add_convert_fusion.2
  11.0 0.1 pad.14.clone
  11.1 0.7 all_to_all.8
  11.8 9.3 %all-to-all-start = ((f32[32,1,512]{2,1,0:T(1,128)}), f32[32,1,512]{2,1,0:T(1,128)S(1)}, u32[]{:S(2)}, u32[]{:S(2)}) async-start(f32[32,1,512]{2,1,0:T(1,128)} %all_to_all.8), calls=%async_computation | async-start | bytes 131072 | tf_op jit(solution)/shard_map/all_to_all | solution.py:571
  21.1 0.7 reshape.130.gain_ref
  21.9 4.9 %all-to-all-done = f32[32,1,512]{2,1,0:T(1,128)S(1)} async-done(((f32[32,1,512]{2,1,0:T(1,128)}), f32[32,1,512]{2,1,0:T(1,128)S(1)}, u32[]{:S(2)}, u32[]{:S(2)}) %all-to-all-start) | async-done | bytes 65568 | tf_op jit(solution)/shard_map/all_to_all | solution.py:571
  26.8 0.2 reshape.131.parts_ref
  26.9 0.7 copy-done.7
  27.6 0.7 place.1
  28.3 4.2 %collective-permute-start = (f32[16,384]{1,0:T(8,128)S(1)}, f32[16,384]{1,0:T(8,128)S(1)}, u32[]{:S(2)}, u32[]{:S(2)}) collective-permute-start(f32[16,384]{1,0:T(8,128)S(1)} %place.1), channel_id=1, source_target_pairs={{0,1},{1,0},{2,3},{3,2},{4,5},{5,4},{6,7},{7,6},{8,9},{9,8},{10,11... | collective-permute-start | bytes 73736 | tf_op jit(solution)/shard_map/ppermute | solution.py:579
  32.5 0.1 compare_and_fusion.1
  32.6 1.2 convert_reduce_fusion
  33.8 0.3 select_reduce_fusion
  34.1 1.2 collective-permute-done
  35.3 1.2 collective-permute-start.1
  36.5 1.9 %collective-permute-done.1 = f32[16,384]{1,0:T(8,128)S(1)} collective-permute-done((f32[16,384]{1,0:T(8,128)S(1)}, f32[16,384]{1,0:T(8,128)S(1)}, u32[]{:S(2)}, u32[]{:S(2)}) %collective-permute-start.1) | collective-permute-done | bytes 24608 | tf_op jit(solution)/shard_map/ppermute | solution.py:579
  38.4 2.8 %collective-permute-start.2 = (f32[16,384]{1,0:T(8,128)S(1)}, f32[16,384]{1,0:T(8,128)S(1)}, u32[]{:S(2)}, u32[]{:S(2)}) collective-permute-start(f32[16,384]{1,0:T(8,128)S(1)} %add.135), channel_id=1, source_target_pairs={{0,4},{1,5},{2,6},{3,7},{4,0},{5,1},{6,2},{7,3},{8,12},{9,13},{10,... | collective-permute-start | bytes 73736 | tf_op jit(solution)/shard_map/ppermute | solution.py:579
  41.1 1.0 and_reduce_fusion
  42.2 0.1 copy.20
  42.3 0.1 reshape.132.code_ref
  42.4 0.4 collective-permute-done.2
  42.7 0.7 add_add_fusion.latent_ref
  43.5 2.0 %copy-done = bf16[320,5120]{1,0:T(8,128)(2,1)S(1)} copy-done((bf16[320,5120]{1,0:T(8,128)(2,1)S(1)}, bf16[320,5120]{1,0:T(8,128)(2,1)}, u32[]{:S(2)}) %copy-start) | copy-done | bytes 3276824
  45.5 0.9 copy-done.2
  46.4 4.2 %hidden.1 = bf16[320,5120]{1,0:T(8,128)(2,1)S(1)} custom-call(f32[16,384]{1,0:T(8,128)S(1)} %add_add_fusion.latent_ref, bf16[16,5120]{1,0:T(8,128)(2,1)S(1)} %copy-done.2, bf16[320,5120]{1,0:T(8,128)(2,1)S(1)} %copy-done, bf16[1,5120]{1,0:T(2,128)(2,1)S(1)} %reshape.130.gain_ref), custom_call_target="tpu_custom_call" | custom-call | tf_op jit(solution)/shard_map/hidden/pallas_call | solution.py:164
  50.6 30.2 %all-gather.2.cloned.1.call-done = bf16[5120,768]{1,0:T(8,128)(2,1)} async-done(((bf16[160,768]{1,0:T(8,128)(2,1)}), bf16[5120,768]{1,0:T(8,128)(2,1)}) %all-gather.2.cloned.1.call-update) | async-done | bytes 7864336 | tf_op jit(solution)/shard_map/all_gather | solution.py:563
  80.8 2.9 %fusion.7.kv_ref.rest_0_ = bf16[320,256]{1,0:T(8,128)(2,1)S(1)} fusion(bf16[320,5120]{1,0:T(8,128)(2,1)S(1)} %hidden.1, bf16[5120,768]{1,0:T(8,128)(2,1)} %all-gather.2.cloned.1.call-done), kind=kOutput, calls=%fused_computation.5 | convolution fusion | flops 838942720 | bytes 6062080 | tf_op jit(solution)/shard_map/dot_general | solution.py:500
  83.7 1.6 %collective-permute-start.3 = (bf16[320,256]{1,0:T(8,128)(2,1)S(1)}, bf16[320,256]{1,0:T(8,128)(2,1)S(1)}, u32[]{:S(2)}, u32[]{:S(2)}) collective-permute-start(bf16[320,256]{1,0:T(8,128)(2,1)S(1)} %fusion.7.kv_ref.rest_0_), channel_id=1, source_target_pairs={{0,16},{8,24},{16,32},{24,40},{32,48},{40,56},{48,0},{56,8},{64,80... | collective-permute-start | bytes 491528 | tf_op jit(solution)/shard_map/ppermute | solution.py:471
  85.3 1.7 %collective-permute-start.4 = (bf16[320,256]{1,0:T(8,128)(2,1)S(1)}, bf16[320,256]{1,0:T(8,128)(2,1)}, u32[]{:S(2)}, u32[]{:S(2)}) collective-permute-start(bf16[320,256]{1,0:T(8,128)(2,1)S(1)} %fusion.7.kv_ref.rest_0_), channel_id=1, source_target_pairs={{0,48},{8,56},{16,0},{24,8},{32,16},{40,24},{48,32},{56,40},{64,11... | collective-permute-start | bytes 491528 | tf_op jit(solution)/shard_map/ppermute | solution.py:471
  87.1 4.1 %collective-permute-done.3.rest_0_.rest_1_ = bf16[320,256]{1,0:T(8,128)(2,1)S(1)} collective-permute-done((bf16[320,256]{1,0:T(8,128)(2,1)S(1)}, bf16[320,256]{1,0:T(8,128)(2,1)S(1)}, u32[]{:S(2)}, u32[]{:S(2)}) %collective-permute-start.3) | collective-permute-done | bytes 163872 | tf_op jit(solution)/shard_map/ppermute | solution.py:471
  91.2 3.6 %collective-permute-done.4.rest_1_.rest_3_ = bf16[320,256]{1,0:T(8,128)(2,1)} collective-permute-done((bf16[320,256]{1,0:T(8,128)(2,1)S(1)}, bf16[320,256]{1,0:T(8,128)(2,1)}, u32[]{:S(2)}, u32[]{:S(2)}) %collective-permute-start.4) | collective-permute-done | bytes 163872 | tf_op jit(solution)/shard_map/ppermute | solution.py:471
  94.8 2.6 %fusion.4.own_ref = bf16[320,512]{1,0:T(8,128)(2,1)} fusion(bf16[320,5120]{1,0:T(8,128)(2,1)S(1)} %hidden.1, bf16[5120,768]{1,0:T(8,128)(2,1)S(1)} %copy-done.8), kind=kOutput, calls=%fused_computation.4 | convolution fusion | flops 1677885440 | bytes 8847360 | tf_op jit(solution)/shard_map/dot_general | solution.py:500
  97.4 0.8 collective-permute-start.5
  98.2 0.7 collective-permute-start.6
  98.9 0.8 collective-permute-start.7
  99.7 0.1 add_convert_fusion.flag_ref
  99.7 1.9 %collective-permute-start.8 = (bf16[320,256]{1,0:T(8,128)(2,1)}, bf16[320,256]{1,0:T(8,128)(2,1)S(1)}, u32[]{:S(2)}, u32[]{:S(2)}) collective-permute-start(bf16[320,256]{1,0:T(8,128)(2,1)} %copy-done.3), channel_id=1, source_target_pairs={{0,128},{8,136},{16,144},{24,152},{32,160},{40,168},{48,176},{56,1... | collective-permute-start | bytes 491528 | tf_op jit(solution)/shard_map/ppermute | solution.py:467
  101.6 0.9 pad_maximum_fusion
  102.5 0.7 collective-permute-start.10
  103.3 1.0 collective-permute-done.6.rest_0_.rest_4_
  104.3 1.6 %collective-permute-done.7.rest_1_.rest_6_ = bf16[320,256]{1,0:T(8,128)(2,1)S(1)} collective-permute-done((bf16[320,256]{1,0:T(8,128)(2,1)}, bf16[320,256]{1,0:T(8,128)(2,1)S(1)}, u32[]{:S(2)}, u32[]{:S(2)}) %collective-permute-start.7) | collective-permute-done | bytes 163872 | tf_op jit(solution)/shard_map/ppermute | solution.py:467
  105.9 1.4 collective-permute-start.12
  107.3 4.0 %collective-permute-start.9 = (bf16[320,256]{1,0:T(8,128)(2,1)}, bf16[320,256]{1,0:T(8,128)(2,1)S(1)}, u32[]{:S(2)}, u32[]{:S(2)}) collective-permute-start(bf16[320,256]{1,0:T(8,128)(2,1)} %copy-done.3), channel_id=1, source_target_pairs={{0,32},{8,40},{16,48},{24,56},{32,0},{40,8},{48,16},{56,24},{64,96... | collective-permute-start | bytes 491528 | tf_op jit(solution)/shard_map/ppermute | solution.py:471
  111.4 0.9 copy-done.4
  112.4 3.0 %first.1 = (f32[136,2560]{1,0:T(8,128)S(1)}, bf16[2560,128]{1,0:T(8,128)(2,1)S(1)}) custom-call(s32[1]{0:T(128)} %bitcast.3.core_ref, bf16[320,512]{1,0:T(8,128)(2,1)} %fusion.4.own_ref, bf16[320,512]{1,0:T(8,128)(2,1)S(1)} %collective-permute-done.5.pair_ref, bf16[320,256]{1,0:T(8,128)(2,1)S(1)} %copy-done.4), custom_call_target="tpu_custom_call" | custom-call | flops 419430400 | bytes 3145728 | tf_op jit(solution)/shard_map/first/pallas_call | solution.py:292
  115.4 5.8 %more.4.state_ref = f32[136,2560]{1,0:T(8,128)S(1)} custom-call(s32[3]{0:T(128)S(1)} %add_convert_fusion.flag_ref, bf16[2560,128]{1,0:T(8,128)(2,1)S(1)} %get-tuple-element.38.q_ref, f32[136,2560]{1,0:T(8,128)S(1)} %get-tuple-element.39.state_ref, bf16[320,256]{1,0:T(8,128)(2,1)S(1)} %collective-permute-done.6.rest_0_.rest_4_, ...), custom_call_target="tpu_custom_call" | custom-call | flops 1258291200 | bytes 3145728 | tf_op jit(solution)/shard_map/more/pallas_call | solution.py:360
  121.2 0.1 collective-permute-start.13
  121.3 1.5 collective-permute-start.14
  122.7 1.7 %more.5.state_ref = f32[136,2560]{1,0:T(8,128)S(1)} custom-call(s32[3]{0:T(128)S(1)} %add_convert_fusion.1.flag_ref, bf16[2560,128]{1,0:T(8,128)(2,1)S(1)} %get-tuple-element.38.q_ref, f32[136,2560]{1,0:T(8,128)S(1)} %more.4.state_ref, bf16[320,256]{1,0:T(8,128)(2,1)S(1)} %collective-permute-done.3.rest_0_.rest_1_, ...), custom_call_target="tpu_custom_call" | custom-call | flops 1258291200 | bytes 3145728 | tf_op jit(solution)/shard_map/more/pallas_call | solution.py:360
  124.4 0.5 collective-permute-start.15
  125.0 9.5 %more.6.state_ref = f32[136,2560]{1,0:T(8,128)S(1)} custom-call(s32[3]{0:T(128)S(1)} %add_convert_fusion.flag_ref, bf16[2560,128]{1,0:T(8,128)(2,1)S(1)} %get-tuple-element.38.q_ref, f32[136,2560]{1,0:T(8,128)S(1)} %more.5.state_ref, bf16[640,256]{1,0:T(8,128)(2,1)S(1)} %collective-permute-done.10.rest_0_.rest_7_, ...), custom_call_target="tpu_custom_call" | custom-call | flops 2516582400 | bytes 3145728 | tf_op jit(solution)/shard_map/more/pallas_call | solution.py:360
  134.5 5.8 %more.7 = (f32[136,1280]{1,0:T(8,128)S(1)}, f32[136,1280]{1,0:T(8,128)S(1)}) custom-call(s32[3]{0:T(128)S(1)} %add_convert_fusion.flag_ref, bf16[2560,128]{1,0:T(8,128)(2,1)S(1)} %get-tuple-element.38.q_ref, f32[136,2560]{1,0:T(8,128)S(1)} %more.6.state_ref, bf16[320,256]{1,0:T(8,128)(2,1)S(1)} %collective-permute-done.13.rest_0_.rest_10_, ...), custom_call_target="tpu_custom_call" | custom-call | flops 1258291200 | bytes 3145728 | tf_op jit(solution)/shard_map/more/pallas_call | solution.py:360
  140.3 3.4 %collective-permute-start.16 = (f32[136,1280]{1,0:T(8,128)S(1)}, f32[136,1280]{1,0:T(8,128)S(1)}, u32[]{:S(2)}, u32[]{:S(2)}) collective-permute-start(f32[136,1280]{1,0:T(8,128)S(1)} %get-tuple-element.55), channel_id=1, source_target_pairs={{0,8},{8,0},{16,24},{24,16},{32,40},{40,32},{48,56},{56,48},{64,72... | collective-permute-start | bytes 2088968 | tf_op jit(solution)/shard_map/ppermute | solution.py:475
  143.7 0.1 pad_add_fusion.place_ref
  143.8 3.9 %pages.1 = (bf16[320,256]{1,0:T(8,128)(2,1)S(1)}, bf16[320,256]{1,0:T(8,128)(2,1)S(1)}) custom-call(s32[3]{0:T(128)S(1)} %pad_add_fusion.place_ref, s32[192]{0:T(256)S(1)} %reshape.132.code_ref, bf16[320,256]{1,0:T(8,128)(2,1)S(1)} %copy-done.5, bf16[320,256]{1,0:T(8,128)(2,1)S(1)} %collective-permute-done.3.rest_0_.rest_1_, ...), custom_call_target="tpu_custom_call" | custom-call | tf_op jit(solution)/shard_map/pages/pallas_call | solution.py:441
  147.7 0.1 collective-permute-start.17
  147.8 0.9 finish.1
  148.8 0.4 collective-permute-done.17
  149.2 0.9 broadcast_select_fusion
  (41 shorter events, 0.4 us)
Async XLA Ops:
  7.2 73.6 %all-gather.2.cloned.1.call-start = ((), (), s32[]{:S(2)}) async-start(), calls=%async_computation.1 | async-start | bytes 8110080 | tf_op jit(solution)/shard_map/all_gather | solution.py:563
  7.9 1.0 copy-start.1
  8.9 0.8 copy-start.6
  11.8 14.9 %all-to-all-start = ((f32[32,1,512]{2,1,0:T(1,128)}), f32[32,1,512]{2,1,0:T(1,128)S(1)}, u32[]{:S(2)}, u32[]{:S(2)}) async-start(f32[32,1,512]{2,1,0:T(1,128)} %all_to_all.8), calls=%async_computation | async-start | bytes 131072 | tf_op jit(solution)/shard_map/all_to_all | solution.py:571
  26.9 0.7 copy-start.7
  28.3 7.0 %collective-permute-start = (f32[16,384]{1,0:T(8,128)S(1)}, f32[16,384]{1,0:T(8,128)S(1)}, u32[]{:S(2)}, u32[]{:S(2)}) collective-permute-start(f32[16,384]{1,0:T(8,128)S(1)} %place.1), channel_id=1, source_target_pairs={{0,1},{1,0},{2,3},{3,2},{4,5},{5,4},{6,7},{7,6},{8,9},{9,8},{10,11... | collective-permute-start | bytes 73736 | tf_op jit(solution)/shard_map/ppermute | solution.py:579
  35.3 3.1 %collective-permute-start.1 = (f32[16,384]{1,0:T(8,128)S(1)}, f32[16,384]{1,0:T(8,128)S(1)}, u32[]{:S(2)}, u32[]{:S(2)}) collective-permute-start(f32[16,384]{1,0:T(8,128)S(1)} %add.134), channel_id=1, source_target_pairs={{0,2},{1,3},{2,0},{3,1},{4,6},{5,7},{6,4},{7,5},{8,10},{9,11},{10,... | collective-permute-start | bytes 73736 | tf_op jit(solution)/shard_map/ppermute | solution.py:579
  38.4 4.4 %collective-permute-start.2 = (f32[16,384]{1,0:T(8,128)S(1)}, f32[16,384]{1,0:T(8,128)S(1)}, u32[]{:S(2)}, u32[]{:S(2)}) collective-permute-start(f32[16,384]{1,0:T(8,128)S(1)} %add.135), channel_id=1, source_target_pairs={{0,4},{1,5},{2,6},{3,7},{4,0},{5,1},{6,2},{7,3},{8,12},{9,13},{10,... | collective-permute-start | bytes 73736 | tf_op jit(solution)/shard_map/ppermute | solution.py:579
  43.5 2.0 %copy-start = (bf16[320,5120]{1,0:T(8,128)(2,1)S(1)}, bf16[320,5120]{1,0:T(8,128)(2,1)}, u32[]{:S(2)}) copy-start(bf16[320,5120]{1,0:T(8,128)(2,1)} %table_ref.1) | copy-start | bytes 9830404
  45.5 0.9 copy-start.2
  80.8 14.0 %copy-start.8 = (bf16[5120,768]{1,0:T(8,128)(2,1)S(1)}, bf16[5120,768]{1,0:T(8,128)(2,1)}, u32[]{:S(2)}) copy-start(bf16[5120,768]{1,0:T(8,128)(2,1)} %all-gather.2.cloned.1.call-done) | copy-start | bytes 23592964
  83.7 7.5 %copy-start.3 = (bf16[320,256]{1,0:T(8,128)(2,1)}, bf16[320,256]{1,0:T(8,128)(2,1)S(1)}, u32[]{:S(2)}) copy-start(bf16[320,256]{1,0:T(8,128)(2,1)S(1)} %fusion.7.kv_ref.rest_0_) | copy-start | bytes 491524
  83.7 7.4 %collective-permute-start.3 = (bf16[320,256]{1,0:T(8,128)(2,1)S(1)}, bf16[320,256]{1,0:T(8,128)(2,1)S(1)}, u32[]{:S(2)}, u32[]{:S(2)}) collective-permute-start(bf16[320,256]{1,0:T(8,128)(2,1)S(1)} %fusion.7.kv_ref.rest_0_), channel_id=1, source_target_pairs={{0,16},{8,24},{16,32},{24,40},{32,48},{40,56},{48,0},{56,8},{64,80... | collective-permute-start | bytes 491528 | tf_op jit(solution)/shard_map/ppermute | solution.py:471
  85.3 9.4 %collective-permute-start.4 = (bf16[320,256]{1,0:T(8,128)(2,1)S(1)}, bf16[320,256]{1,0:T(8,128)(2,1)}, u32[]{:S(2)}, u32[]{:S(2)}) collective-permute-start(bf16[320,256]{1,0:T(8,128)(2,1)S(1)} %fusion.7.kv_ref.rest_0_), channel_id=1, source_target_pairs={{0,48},{8,56},{16,0},{24,8},{32,16},{40,24},{48,32},{56,40},{64,11... | collective-permute-start | bytes 491528 | tf_op jit(solution)/shard_map/ppermute | solution.py:471
  97.4 9.9 %collective-permute-start.5 = (bf16[320,512]{1,0:T(8,128)(2,1)}, bf16[320,512]{1,0:T(8,128)(2,1)S(1)}, u32[]{:S(2)}, u32[]{:S(2)}) collective-permute-start(bf16[320,512]{1,0:T(8,128)(2,1)} %fusion.4.own_ref), channel_id=1, source_target_pairs={{0,8},{8,0},{16,24},{24,16},{32,40},{40,32},{48,56},{56,48},{64,72... | collective-permute-start | bytes 983048 | tf_op jit(solution)/shard_map/ppermute | solution.py:475
  98.2 6.0 %collective-permute-start.6 = (bf16[320,256]{1,0:T(8,128)(2,1)}, bf16[320,256]{1,0:T(8,128)(2,1)S(1)}, u32[]{:S(2)}, u32[]{:S(2)}) collective-permute-start(bf16[320,256]{1,0:T(8,128)(2,1)} %copy-done.3), channel_id=1, source_target_pairs={{0,64},{8,72},{16,80},{24,88},{32,96},{40,104},{48,112},{56,120},{... | collective-permute-start | bytes 491528 | tf_op jit(solution)/shard_map/ppermute | solution.py:467
  98.9 7.0 %collective-permute-start.7 = (bf16[320,256]{1,0:T(8,128)(2,1)}, bf16[320,256]{1,0:T(8,128)(2,1)S(1)}, u32[]{:S(2)}, u32[]{:S(2)}) collective-permute-start(bf16[320,256]{1,0:T(8,128)(2,1)} %copy-done.3), channel_id=1, source_target_pairs={{0,192},{8,200},{16,208},{24,216},{32,224},{40,232},{48,240},{56,2... | collective-permute-start | bytes 491528 | tf_op jit(solution)/shard_map/ppermute | solution.py:467
  99.7 15.6 %collective-permute-start.8 = (bf16[320,256]{1,0:T(8,128)(2,1)}, bf16[320,256]{1,0:T(8,128)(2,1)S(1)}, u32[]{:S(2)}, u32[]{:S(2)}) collective-permute-start(bf16[320,256]{1,0:T(8,128)(2,1)} %copy-done.3), channel_id=1, source_target_pairs={{0,128},{8,136},{16,144},{24,152},{32,160},{40,168},{48,176},{56,1... | collective-permute-start | bytes 491528 | tf_op jit(solution)/shard_map/ppermute | solution.py:467
  102.5 21.9 %collective-permute-start.10 = (bf16[640,256]{1,0:T(8,128)(2,1)S(1)}, bf16[640,256]{1,0:T(8,128)(2,1)S(1)}, u32[]{:S(2)}, u32[]{:S(2)}) collective-permute-start(bf16[640,256]{1,0:T(8,128)(2,1)S(1)} %pad_maximum_fusion), channel_id=1, source_target_pairs={{0,64},{8,72},{16,80},{24,88},{32,96},{40,104},{48,112},{56,120},{... | collective-permute-start | bytes 983048 | tf_op jit(solution)/shard_map/ppermute | solution.py:467
  104.2 20.7 %collective-permute-start.11 = (bf16[640,256]{1,0:T(8,128)(2,1)S(1)}, bf16[640,256]{1,0:T(8,128)(2,1)S(1)}, u32[]{:S(2)}, u32[]{:S(2)}) collective-permute-start(bf16[640,256]{1,0:T(8,128)(2,1)S(1)} %pad_maximum_fusion), channel_id=1, source_target_pairs={{0,192},{8,200},{16,208},{24,216},{32,224},{40,232},{48,240},{56,2... | collective-permute-start | bytes 983048 | tf_op jit(solution)/shard_map/ppermute | solution.py:467
  105.9 19.1 %collective-permute-start.12 = (bf16[640,256]{1,0:T(8,128)(2,1)S(1)}, bf16[640,256]{1,0:T(8,128)(2,1)S(1)}, u32[]{:S(2)}, u32[]{:S(2)}) collective-permute-start(bf16[640,256]{1,0:T(8,128)(2,1)S(1)} %pad_maximum_fusion), channel_id=1, source_target_pairs={{0,128},{8,136},{16,144},{24,152},{32,160},{40,168},{48,176},{56,1... | collective-permute-start | bytes 983048 | tf_op jit(solution)/shard_map/ppermute | solution.py:467
  107.3 13.8 %collective-permute-start.9 = (bf16[320,256]{1,0:T(8,128)(2,1)}, bf16[320,256]{1,0:T(8,128)(2,1)S(1)}, u32[]{:S(2)}, u32[]{:S(2)}) collective-permute-start(bf16[320,256]{1,0:T(8,128)(2,1)} %copy-done.3), channel_id=1, source_target_pairs={{0,32},{8,40},{16,48},{24,56},{32,0},{40,8},{48,16},{56,24},{64,96... | collective-permute-start | bytes 491528 | tf_op jit(solution)/shard_map/ppermute | solution.py:471
  111.4 0.9 copy-start.4
  121.2 13.3 %collective-permute-start.13 = (bf16[320,256]{1,0:T(8,128)(2,1)S(1)}, bf16[320,256]{1,0:T(8,128)(2,1)S(1)}, u32[]{:S(2)}, u32[]{:S(2)}) collective-permute-start(bf16[320,256]{1,0:T(8,128)(2,1)S(1)} %collective-permute-done.9.rest_2_), channel_id=1, source_target_pairs={{0,64},{8,72},{16,80},{24,88},{32,96},{40,104},{48,112},{56,120},{... | collective-permute-start | bytes 491528 | tf_op jit(solution)/shard_map/ppermute | solution.py:467
  121.3 13.2 %collective-permute-start.14 = (bf16[320,256]{1,0:T(8,128)(2,1)S(1)}, bf16[320,256]{1,0:T(8,128)(2,1)S(1)}, u32[]{:S(2)}, u32[]{:S(2)}) collective-permute-start(bf16[320,256]{1,0:T(8,128)(2,1)S(1)} %collective-permute-done.9.rest_2_), channel_id=1, source_target_pairs={{0,192},{8,200},{16,208},{24,216},{32,224},{40,232},{48,240},{56,2... | collective-permute-start | bytes 491528 | tf_op jit(solution)/shard_map/ppermute | solution.py:467
  124.4 10.1 %collective-permute-start.15 = (bf16[320,256]{1,0:T(8,128)(2,1)S(1)}, bf16[320,256]{1,0:T(8,128)(2,1)S(1)}, u32[]{:S(2)}, u32[]{:S(2)}) collective-permute-start(bf16[320,256]{1,0:T(8,128)(2,1)S(1)} %collective-permute-done.9.rest_2_), channel_id=1, source_target_pairs={{0,128},{8,136},{16,144},{24,152},{32,160},{40,168},{48,176},{56,1... | collective-permute-start | bytes 491528 | tf_op jit(solution)/shard_map/ppermute | solution.py:467
  134.4 9.4 %copy-start.5 = (bf16[320,256]{1,0:T(8,128)(2,1)S(1)}, bf16[320,256]{1,0:T(8,128)(2,1)}, u32[]{:S(2)}) copy-start(bf16[320,256]{1,0:T(8,128)(2,1)} %copy-done.3) | copy-start | bytes 491524
  140.3 7.5 %collective-permute-start.16 = (f32[136,1280]{1,0:T(8,128)S(1)}, f32[136,1280]{1,0:T(8,128)S(1)}, u32[]{:S(2)}, u32[]{:S(2)}) collective-permute-start(f32[136,1280]{1,0:T(8,128)S(1)} %get-tuple-element.55), channel_id=1, source_target_pairs={{0,8},{8,0},{16,24},{24,16},{32,40},{40,32},{48,56},{56,48},{64,72... | collective-permute-start | bytes 2088968 | tf_op jit(solution)/shard_map/ppermute | solution.py:475
  147.7 1.5 collective-permute-start.17
Sparse Core Ops, SparseCore 0:
  9.9 70.8 all-gather.1

commit v2 on v0

--- a/solution.py
+++ b/solution.py
@@ -396,6 +396,21 @@
     )(own, got)
 
 
+def take_pages(group, owner, entry, base, code_ref, array, held_ref):
+    code = code_ref[group * MOST + entry]
+
+    @pl.when(code >= 0)
+    def _():
+        page = code >> 6
+        slot = (code & 63) + owner * PAGES
+        row = pl.multiple_of(base + (page >> 1) * 2 * PAGE, 2 * PAGE)
+        rows = array[pl.ds(row, 2 * PAGE), :].astype(jnp.float32)
+        rows = jnp.where((page & 1) == 1, rows[PAGE:], rows[:PAGE])
+        held_ref[pl.ds(pl.multiple_of(slot * PAGE, PAGE), PAGE), :] = rows
+        if entry + 1 < MOST:
+            take_pages(group, owner, entry + 1, base, code_ref, array, held_ref)
+
+
 def page_kernel(place_ref, code_ref, *rest):
     count = (len(rest) - 4) // 2
     remote, own_ref, pair_ref = rest[:count], rest[count], rest[count + 1]
@@ -420,17 +435,8 @@
                 waited.add(index)
             array = arrays[index]
             source = (((y - by_y) & 3) * 4 + ((z - by_z) & 3)) * 2 + core
-            for entry in range(2 * MOST):
-                code = code_ref[source * 2 * MOST + entry]
-
-                @pl.when(code >= 0)
-                def _():
-                    page = code >> 6
-                    slot = (code & 63) + entry // MOST * PAGES
-                    row = pl.multiple_of(base + (page >> 1) * 2 * PAGE, 2 * PAGE)
-                    rows = array[pl.ds(row, 2 * PAGE), :].astype(jnp.float32)
-                    rows = jnp.where((page & 1) == 1, rows[PAGE:], rows[:PAGE])
-                    held_ref[pl.ds(pl.multiple_of(slot * PAGE, PAGE), PAGE), :] = rows
+            for owner in range(2):
+                take_pages(source * 2 + owner, owner, 0, base, code_ref, array, held_ref)
 
     own_ref[...] = held_ref[: PAGES * PAGE].astype(jnp.bfloat16)
     pair_ref[...] = held_ref[PAGES * PAGE :].astype(jnp.bfloat16)

time: 151 us -> 150 us (level)
  no operation moved by 1% of the time
where the time goes in v2:
time: 150 us; the launch traced here: 148 us
  waiting for transfers between devices  41.7 us (28%)
  starting transfers between devices  37 us (25%)
  Pallas kernels  35.6 us (24%)
  between operations  14.3 us (10%)
  local copies, waits for them, and re-layouts  8.44 us (6%)
  matrix products  5.57 us (4%)
  other arithmetic  5.22 us (3%)
    all_gather x1, waiting for transfers between devices, on_device(): weight = lax.all_gather(qkv_weight, 'seq', axis=0, tiled=True)  30.2 us
    pallas_call x4, Pallas kernels, attend_more(): pl.pallas_call(functools.partial(more_kernel, count, split), in_specs=[pl...  22.5 us
    ppermute x9, starting transfers between devices, along_y(): lax.ppermute(value, 'seq', moves(lambda y, z, c: ((y + count) % 4, z, c)))  12.1 us
    all_to_all x1, starting transfers between devices, on_device(): lax.all_to_all(message, 'seq', split_axis=0, concat_axis=0, tiled=True)  9.26 us
    ppermute x3, starting transfers between devices, on_device(): latent = latent + lax.ppermute(latent, 'tensor', swap)  8.17 us
    unnamed x13, local copies, waits for them, and re-layouts  6.46 us
    dot_general x2, matrix products, project(): jnp.dot(normed, weight, preferred_element_type=jnp.float32)  5.57 us
    all_to_all x1, waiting for transfers between devices, on_device(): lax.all_to_all(message, 'seq', split_axis=0, concat_axis=0, tiled=True)  4.85 us
  transfers between devices with their start and end apart: 20, of which 8 were waited for; matrix products, arithmetic and copies ran while one was open for 4% of the time, Pallas kernels for 20%

profile of v2, /device:TPU:25, one launch (start us, length us, event | category | flops | bytes accessed | tf_op | source)
XLA Modules:
  0.0 147.8 jit_solution(18292402789578869964)
XLA Ops:
  7.2 0.0 all-gather.2.cloned.1.call-start
  7.2 0.7 all-gather.2.cloned.1.call-update
  7.9 1.0 copy-done.1
  8.9 0.8 copy-done.3
  9.7 0.5 conv.1
  10.2 0.1 reshape.129
  10.3 0.7 add_convert_fusion.2
  11.0 0.1 pad.14.clone
  11.1 0.7 all_to_all.8
  11.8 9.3 %all-to-all-start = ((f32[32,1,512]{2,1,0:T(1,128)}), f32[32,1,512]{2,1,0:T(1,128)S(1)}, u32[]{:S(2)}, u32[]{:S(2)}) async-start(f32[32,1,512]{2,1,0:T(1,128)} %all_to_all.8), calls=%async_computation | async-start | bytes 131072 | tf_op jit(solution)/shard_map/all_to_all | solution.py:577
  21.1 0.7 reshape.130.gain_ref
  21.9 4.9 %all-to-all-done = f32[32,1,512]{2,1,0:T(1,128)S(1)} async-done(((f32[32,1,512]{2,1,0:T(1,128)}), f32[32,1,512]{2,1,0:T(1,128)S(1)}, u32[]{:S(2)}, u32[]{:S(2)}) %all-to-all-start) | async-done | bytes 65568 | tf_op jit(solution)/shard_map/all_to_all | solution.py:577
  26.8 0.2 reshape.131.parts_ref
  26.9 0.7 copy-done.4
  27.6 0.7 place.1
  28.3 4.2 %collective-permute-start = (f32[16,384]{1,0:T(8,128)S(1)}, f32[16,384]{1,0:T(8,128)S(1)}, u32[]{:S(2)}, u32[]{:S(2)}) collective-permute-start(f32[16,384]{1,0:T(8,128)S(1)} %place.1), channel_id=1, source_target_pairs={{0,1},{1,0},{2,3},{3,2},{4,5},{5,4},{6,7},{7,6},{8,9},{9,8},{10,11... | collective-permute-start | bytes 73736 | tf_op jit(solution)/shard_map/ppermute | solution.py:585
  32.5 0.1 compare_and_fusion.1
  32.6 1.2 convert_reduce_fusion
  33.8 0.3 select_reduce_fusion
  34.0 0.1 slice_convert_fusion
  34.1 1.2 collective-permute-done
  35.3 1.2 collective-permute-start.1
  36.5 1.9 %collective-permute-done.1 = f32[16,384]{1,0:T(8,128)S(1)} collective-permute-done((f32[16,384]{1,0:T(8,128)S(1)}, f32[16,384]{1,0:T(8,128)S(1)}, u32[]{:S(2)}, u32[]{:S(2)}) %collective-permute-start.1) | collective-permute-done | bytes 24608 | tf_op jit(solution)/shard_map/ppermute | solution.py:585
  38.4 2.8 %collective-permute-start.2 = (f32[16,384]{1,0:T(8,128)S(1)}, f32[16,384]{1,0:T(8,128)S(1)}, u32[]{:S(2)}, u32[]{:S(2)}) collective-permute-start(f32[16,384]{1,0:T(8,128)S(1)} %add.135), channel_id=1, source_target_pairs={{0,4},{1,5},{2,6},{3,7},{4,0},{5,1},{6,2},{7,3},{8,12},{9,13},{10,... | collective-permute-start | bytes 73736 | tf_op jit(solution)/shard_map/ppermute | solution.py:585
  41.1 1.0 and_reduce_fusion
  42.2 0.1 copy.20
  42.3 0.1 reshape.132.code_ref
  42.4 0.4 collective-permute-done.2
  42.7 0.7 add_add_fusion.latent_ref
  43.5 2.0 %copy-done = bf16[320,5120]{1,0:T(8,128)(2,1)S(1)} copy-done((bf16[320,5120]{1,0:T(8,128)(2,1)S(1)}, bf16[320,5120]{1,0:T(8,128)(2,1)}, u32[]{:S(2)}) %copy-start) | copy-done | bytes 3276824
  45.5 0.9 copy-done.2
  46.4 4.2 %hidden.1 = bf16[320,5120]{1,0:T(8,128)(2,1)S(1)} custom-call(f32[16,384]{1,0:T(8,128)S(1)} %add_add_fusion.latent_ref, bf16[16,5120]{1,0:T(8,128)(2,1)S(1)} %copy-done.2, bf16[320,5120]{1,0:T(8,128)(2,1)S(1)} %copy-done, bf16[1,5120]{1,0:T(2,128)(2,1)S(1)} %reshape.130.gain_ref), custom_call_target="tpu_custom_call" | custom-call | tf_op jit(solution)/shard_map/hidden/pallas_call | solution.py:164
  50.6 30.2 %all-gather.2.cloned.1.call-done = bf16[5120,768]{1,0:T(8,128)(2,1)} async-done(((bf16[160,768]{1,0:T(8,128)(2,1)}), bf16[5120,768]{1,0:T(8,128)(2,1)}) %all-gather.2.cloned.1.call-update) | async-done | bytes 7864336 | tf_op jit(solution)/shard_map/all_gather | solution.py:569
  80.8 2.9 %fusion.7.kv_ref.rest_0_ = bf16[320,256]{1,0:T(8,128)(2,1)S(1)} fusion(bf16[320,5120]{1,0:T(8,128)(2,1)S(1)} %hidden.1, bf16[5120,768]{1,0:T(8,128)(2,1)} %all-gather.2.cloned.1.call-done), kind=kOutput, calls=%fused_computation.5 | convolution fusion | flops 838942720 | bytes 6062080 | tf_op jit(solution)/shard_map/dot_general | solution.py:506
  83.7 1.1 copy-done.5
  84.8 2.6 %fusion.4.own_ref = bf16[320,512]{1,0:T(8,128)(2,1)} fusion(bf16[320,5120]{1,0:T(8,128)(2,1)S(1)} %hidden.1, bf16[5120,768]{1,0:T(8,128)(2,1)S(1)} %copy-done.5), kind=kOutput, calls=%fused_computation.4 | convolution fusion | flops 1677885440 | bytes 8847360 | tf_op jit(solution)/shard_map/dot_general | solution.py:506
  87.4 0.3 collective-permute-start.3
  87.7 2.4 %collective-permute-start.5 = (bf16[320,256]{1,0:T(8,128)(2,1)S(1)}, bf16[320,256]{1,0:T(8,128)(2,1)S(1)}, u32[]{:S(2)}, u32[]{:S(2)}) collective-permute-start(bf16[320,256]{1,0:T(8,128)(2,1)S(1)} %fusion.7.kv_ref.rest_0_), channel_id=1, source_target_pairs={{0,48},{8,56},{16,0},{24,8},{32,16},{40,24},{48,32},{56,40},{64,11... | collective-permute-start | bytes 491528 | tf_op jit(solution)/shard_map/ppermute | solution.py:477
  90.1 1.3 collective-permute-start.8
  91.4 0.5 collective-permute-start.7
  91.9 0.1 add_convert_fusion.flag_ref
  92.0 2.3 %collective-permute-start.6 = (bf16[320,256]{1,0:T(8,128)(2,1)S(1)}, bf16[320,256]{1,0:T(8,128)(2,1)S(1)}, u32[]{:S(2)}, u32[]{:S(2)}) collective-permute-start(bf16[320,256]{1,0:T(8,128)(2,1)S(1)} %fusion.7.kv_ref.rest_0_), channel_id=1, source_target_pairs={{0,64},{8,72},{16,80},{24,88},{32,96},{40,104},{48,112},{56,120},{... | collective-permute-start | bytes 491528 | tf_op jit(solution)/shard_map/ppermute | solution.py:473
  94.2 3.0 %first.1 = (f32[136,2560]{1,0:T(8,128)S(1)}, bf16[2560,128]{1,0:T(8,128)(2,1)S(1)}) custom-call(s32[1]{0:T(128)} %bitcast.3.core_ref, bf16[320,512]{1,0:T(8,128)(2,1)} %fusion.4.own_ref, bf16[320,512]{1,0:T(8,128)(2,1)S(1)} %collective-permute-done.3.pair_ref, bf16[320,256]{1,0:T(8,128)(2,1)S(1)} %fusion.7.kv_ref.rest_0_), custom_call_target="tpu_custom_call" | custom-call | flops 419430400 | bytes 3145728 | tf_op jit(solution)/shard_map/first/pallas_call | solution.py:292
  97.2 0.5 collective-permute-done.4.rest_0_.rest_1_
  97.8 1.9 %collective-permute-start.12 = (bf16[640,256]{1,0:T(8,128)(2,1)S(1)}, bf16[640,256]{1,0:T(8,128)(2,1)S(1)}, u32[]{:S(2)}, u32[]{:S(2)}) collective-permute-start(bf16[640,256]{1,0:T(8,128)(2,1)S(1)} %pad_maximum_fusion), channel_id=1, source_target_pairs={{0,128},{8,136},{16,144},{24,152},{32,160},{40,168},{48,176},{56,1... | collective-permute-start | bytes 983048 | tf_op jit(solution)/shard_map/ppermute | solution.py:473
  99.6 0.9 collective-permute-start.11
  100.5 1.8 %collective-permute-start.10 = (bf16[640,256]{1,0:T(8,128)(2,1)S(1)}, bf16[640,256]{1,0:T(8,128)(2,1)S(1)}, u32[]{:S(2)}, u32[]{:S(2)}) collective-permute-start(bf16[640,256]{1,0:T(8,128)(2,1)S(1)} %pad_maximum_fusion), channel_id=1, source_target_pairs={{0,64},{8,72},{16,80},{24,88},{32,96},{40,104},{48,112},{56,120},{... | collective-permute-start | bytes 983048 | tf_op jit(solution)/shard_map/ppermute | solution.py:473
  102.3 2.3 %collective-permute-start.9 = (bf16[320,256]{1,0:T(8,128)(2,1)S(1)}, bf16[320,256]{1,0:T(8,128)(2,1)S(1)}, u32[]{:S(2)}, u32[]{:S(2)}) collective-permute-start(bf16[320,256]{1,0:T(8,128)(2,1)S(1)} %fusion.7.kv_ref.rest_0_), channel_id=1, source_target_pairs={{0,32},{8,40},{16,48},{24,56},{32,0},{40,8},{48,16},{56,24},{64,96... | collective-permute-start | bytes 491528 | tf_op jit(solution)/shard_map/ppermute | solution.py:477
  104.6 0.1 add_convert_fusion.1.flag_ref
  104.7 5.7 %more.4.state_ref = f32[136,2560]{1,0:T(8,128)S(1)} custom-call(s32[3]{0:T(128)S(1)} %add_convert_fusion.flag_ref, bf16[2560,128]{1,0:T(8,128)(2,1)S(1)} %get-tuple-element.37.q_ref, f32[136,2560]{1,0:T(8,128)S(1)} %get-tuple-element.39.state_ref, bf16[320,256]{1,0:T(8,128)(2,1)S(1)} %collective-permute-done.6.rest_0_.rest_4_, ...), custom_call_target="tpu_custom_call" | custom-call | flops 1258291200 | bytes 3145728 | tf_op jit(solution)/shard_map/more/pallas_call | solution.py:360
  110.4 1.6 %collective-permute-done.9.rest_2_ = bf16[320,256]{1,0:T(8,128)(2,1)S(1)} collective-permute-done((bf16[320,256]{1,0:T(8,128)(2,1)S(1)}, bf16[320,256]{1,0:T(8,128)(2,1)S(1)}, u32[]{:S(2)}, u32[]{:S(2)}) %collective-permute-start.9) | collective-permute-done | bytes 163872 | tf_op jit(solution)/shard_map/ppermute | solution.py:477
  112.0 0.6 collective-permute-start.15
  112.7 1.3 collective-permute-start.14
  114.0 1.3 more.5.state_ref
  115.4 1.6 %collective-permute-start.13 = (bf16[320,256]{1,0:T(8,128)(2,1)S(1)}, bf16[320,256]{1,0:T(8,128)(2,1)S(1)}, u32[]{:S(2)}, u32[]{:S(2)}) collective-permute-start(bf16[320,256]{1,0:T(8,128)(2,1)S(1)} %collective-permute-done.9.rest_2_), channel_id=1, source_target_pairs={{0,64},{8,72},{16,80},{24,88},{32,96},{40,104},{48,112},{56,120},{... | collective-permute-start | bytes 491528 | tf_op jit(solution)/shard_map/ppermute | solution.py:473
  117.0 9.6 %more.6.state_ref = f32[136,2560]{1,0:T(8,128)S(1)} custom-call(s32[3]{0:T(128)S(1)} %add_convert_fusion.flag_ref, bf16[2560,128]{1,0:T(8,128)(2,1)S(1)} %get-tuple-element.37.q_ref, f32[136,2560]{1,0:T(8,128)S(1)} %more.5.state_ref, bf16[640,256]{1,0:T(8,128)(2,1)S(1)} %collective-permute-done.10.rest_0_.rest_7_, ...), custom_call_target="tpu_custom_call" | custom-call | flops 2516582400 | bytes 3145728 | tf_op jit(solution)/shard_map/more/pallas_call | solution.py:360
  126.6 5.8 %more.7 = (f32[136,1280]{1,0:T(8,128)S(1)}, f32[136,1280]{1,0:T(8,128)S(1)}) custom-call(s32[3]{0:T(128)S(1)} %add_convert_fusion.flag_ref, bf16[2560,128]{1,0:T(8,128)(2,1)S(1)} %get-tuple-element.37.q_ref, f32[136,2560]{1,0:T(8,128)S(1)} %more.6.state_ref, bf16[320,256]{1,0:T(8,128)(2,1)S(1)} %collective-permute-done.13.rest_0_.rest_10_, ...), custom_call_target="tpu_custom_call" | custom-call | flops 1258291200 | bytes 3145728 | tf_op jit(solution)/shard_map/more/pallas_call | solution.py:360
  132.4 2.3 %collective-permute-start.16 = (f32[136,1280]{1,0:T(8,128)S(1)}, f32[136,1280]{1,0:T(8,128)S(1)}, u32[]{:S(2)}, u32[]{:S(2)}) collective-permute-start(f32[136,1280]{1,0:T(8,128)S(1)} %get-tuple-element.55), channel_id=1, source_target_pairs={{0,8},{8,0},{16,24},{24,16},{32,40},{40,32},{48,56},{56,48},{64,72... | collective-permute-start | bytes 2088968 | tf_op jit(solution)/shard_map/ppermute | solution.py:481
  134.7 0.1 pad_add_fusion.place_ref
  134.8 3.7 %pages.1 = (bf16[320,256]{1,0:T(8,128)(2,1)S(1)}, bf16[320,256]{1,0:T(8,128)(2,1)S(1)}) custom-call(s32[3]{0:T(128)S(1)} %pad_add_fusion.place_ref, s32[192]{0:T(256)S(1)} %reshape.132.code_ref, bf16[320,256]{1,0:T(8,128)(2,1)S(1)} %fusion.7.kv_ref.rest_0_, bf16[320,256]{1,0:T(8,128)(2,1)S(1)} %collective-permute-done.4.rest_0_.rest_1_, ...), custom_call_target="tpu_custom_call" | custom-call | tf_op jit(solution)/shard_map/pages/pallas_call | solution.py:447
  138.5 0.1 collective-permute-start.17
  138.6 1.0 finish.1
  139.6 0.4 collective-permute-done.17
  140.0 0.9 broadcast_select_fusion
  (35 shorter events, 0.2 us)
Async XLA Ops:
  7.2 73.6 %all-gather.2.cloned.1.call-start = ((), (), s32[]{:S(2)}) async-start(), calls=%async_computation.1 | async-start | bytes 8110080 | tf_op jit(solution)/shard_map/all_gather | solution.py:569
  7.9 1.0 copy-start.1
  8.9 0.8 copy-start.3
  11.8 14.9 %all-to-all-start = ((f32[32,1,512]{2,1,0:T(1,128)}), f32[32,1,512]{2,1,0:T(1,128)S(1)}, u32[]{:S(2)}, u32[]{:S(2)}) async-start(f32[32,1,512]{2,1,0:T(1,128)} %all_to_all.8), calls=%async_computation | async-start | bytes 131072 | tf_op jit(solution)/shard_map/all_to_all | solution.py:577
  26.9 0.7 copy-start.4
  28.3 7.0 %collective-permute-start = (f32[16,384]{1,0:T(8,128)S(1)}, f32[16,384]{1,0:T(8,128)S(1)}, u32[]{:S(2)}, u32[]{:S(2)}) collective-permute-start(f32[16,384]{1,0:T(8,128)S(1)} %place.1), channel_id=1, source_target_pairs={{0,1},{1,0},{2,3},{3,2},{4,5},{5,4},{6,7},{7,6},{8,9},{9,8},{10,11... | collective-permute-start | bytes 73736 | tf_op jit(solution)/shard_map/ppermute | solution.py:585
  35.3 3.1 %collective-permute-start.1 = (f32[16,384]{1,0:T(8,128)S(1)}, f32[16,384]{1,0:T(8,128)S(1)}, u32[]{:S(2)}, u32[]{:S(2)}) collective-permute-start(f32[16,384]{1,0:T(8,128)S(1)} %add.134), channel_id=1, source_target_pairs={{0,2},{1,3},{2,0},{3,1},{4,6},{5,7},{6,4},{7,5},{8,10},{9,11},{10,... | collective-permute-start | bytes 73736 | tf_op jit(solution)/shard_map/ppermute | solution.py:585
  38.4 4.4 %collective-permute-start.2 = (f32[16,384]{1,0:T(8,128)S(1)}, f32[16,384]{1,0:T(8,128)S(1)}, u32[]{:S(2)}, u32[]{:S(2)}) collective-permute-start(f32[16,384]{1,0:T(8,128)S(1)} %add.135), channel_id=1, source_target_pairs={{0,4},{1,5},{2,6},{3,7},{4,0},{5,1},{6,2},{7,3},{8,12},{9,13},{10,... | collective-permute-start | bytes 73736 | tf_op jit(solution)/shard_map/ppermute | solution.py:585
  43.5 2.0 %copy-start = (bf16[320,5120]{1,0:T(8,128)(2,1)S(1)}, bf16[320,5120]{1,0:T(8,128)(2,1)}, u32[]{:S(2)}) copy-start(bf16[320,5120]{1,0:T(8,128)(2,1)} %table_ref.1) | copy-start | bytes 9830404
  45.5 0.9 copy-start.2
  80.8 4.0 %copy-start.5 = (bf16[5120,768]{1,0:T(8,128)(2,1)S(1)}, bf16[5120,768]{1,0:T(8,128)(2,1)}, u32[]{:S(2)}) copy-start(bf16[5120,768]{1,0:T(8,128)(2,1)} %all-gather.2.cloned.1.call-done) | copy-start | bytes 23592964
  87.4 4.5 %collective-permute-start.3 = (bf16[320,512]{1,0:T(8,128)(2,1)}, bf16[320,512]{1,0:T(8,128)(2,1)S(1)}, u32[]{:S(2)}, u32[]{:S(2)}) collective-permute-start(bf16[320,512]{1,0:T(8,128)(2,1)} %fusion.4.own_ref), channel_id=1, source_target_pairs={{0,8},{8,0},{16,24},{24,16},{32,40},{40,32},{48,56},{56,48},{64,72... | collective-permute-start | bytes 983048 | tf_op jit(solution)/shard_map/ppermute | solution.py:481
  87.7 9.5 %collective-permute-start.5 = (bf16[320,256]{1,0:T(8,128)(2,1)S(1)}, bf16[320,256]{1,0:T(8,128)(2,1)S(1)}, u32[]{:S(2)}, u32[]{:S(2)}) collective-permute-start(bf16[320,256]{1,0:T(8,128)(2,1)S(1)} %fusion.7.kv_ref.rest_0_), channel_id=1, source_target_pairs={{0,48},{8,56},{16,0},{24,8},{32,16},{40,24},{48,32},{56,40},{64,11... | collective-permute-start | bytes 491528 | tf_op jit(solution)/shard_map/ppermute | solution.py:477
  90.1 7.6 %collective-permute-start.4 = (bf16[320,256]{1,0:T(8,128)(2,1)S(1)}, bf16[320,256]{1,0:T(8,128)(2,1)S(1)}, u32[]{:S(2)}, u32[]{:S(2)}) collective-permute-start(bf16[320,256]{1,0:T(8,128)(2,1)S(1)} %fusion.7.kv_ref.rest_0_), channel_id=1, source_target_pairs={{0,16},{8,24},{16,32},{24,40},{32,48},{40,56},{48,0},{56,8},{64,80... | collective-permute-start | bytes 491528 | tf_op jit(solution)/shard_map/ppermute | solution.py:477
  90.1 10.4 %collective-permute-start.8 = (bf16[320,256]{1,0:T(8,128)(2,1)S(1)}, bf16[320,256]{1,0:T(8,128)(2,1)S(1)}, u32[]{:S(2)}, u32[]{:S(2)}) collective-permute-start(bf16[320,256]{1,0:T(8,128)(2,1)S(1)} %fusion.7.kv_ref.rest_0_), channel_id=1, source_target_pairs={{0,128},{8,136},{16,144},{24,152},{32,160},{40,168},{48,176},{56,1... | collective-permute-start | bytes 491528 | tf_op jit(solution)/shard_map/ppermute | solution.py:473
  91.4 10.9 %collective-permute-start.7 = (bf16[320,256]{1,0:T(8,128)(2,1)S(1)}, bf16[320,256]{1,0:T(8,128)(2,1)S(1)}, u32[]{:S(2)}, u32[]{:S(2)}) collective-permute-start(bf16[320,256]{1,0:T(8,128)(2,1)S(1)} %fusion.7.kv_ref.rest_0_), channel_id=1, source_target_pairs={{0,192},{8,200},{16,208},{24,216},{32,224},{40,232},{48,240},{56,2... | collective-permute-start | bytes 491528 | tf_op jit(solution)/shard_map/ppermute | solution.py:473
  92.0 12.7 %collective-permute-start.6 = (bf16[320,256]{1,0:T(8,128)(2,1)S(1)}, bf16[320,256]{1,0:T(8,128)(2,1)S(1)}, u32[]{:S(2)}, u32[]{:S(2)}) collective-permute-start(bf16[320,256]{1,0:T(8,128)(2,1)S(1)} %fusion.7.kv_ref.rest_0_), channel_id=1, source_target_pairs={{0,64},{8,72},{16,80},{24,88},{32,96},{40,104},{48,112},{56,120},{... | collective-permute-start | bytes 491528 | tf_op jit(solution)/shard_map/ppermute | solution.py:473
  97.8 17.6 %collective-permute-start.12 = (bf16[640,256]{1,0:T(8,128)(2,1)S(1)}, bf16[640,256]{1,0:T(8,128)(2,1)S(1)}, u32[]{:S(2)}, u32[]{:S(2)}) collective-permute-start(bf16[640,256]{1,0:T(8,128)(2,1)S(1)} %pad_maximum_fusion), channel_id=1, source_target_pairs={{0,128},{8,136},{16,144},{24,152},{32,160},{40,168},{48,176},{56,1... | collective-permute-start | bytes 983048 | tf_op jit(solution)/shard_map/ppermute | solution.py:473
  99.6 17.4 %collective-permute-start.11 = (bf16[640,256]{1,0:T(8,128)(2,1)S(1)}, bf16[640,256]{1,0:T(8,128)(2,1)S(1)}, u32[]{:S(2)}, u32[]{:S(2)}) collective-permute-start(bf16[640,256]{1,0:T(8,128)(2,1)S(1)} %pad_maximum_fusion), channel_id=1, source_target_pairs={{0,192},{8,200},{16,208},{24,216},{32,224},{40,232},{48,240},{56,2... | collective-permute-start | bytes 983048 | tf_op jit(solution)/shard_map/ppermute | solution.py:473
  100.5 16.5 %collective-permute-start.10 = (bf16[640,256]{1,0:T(8,128)(2,1)S(1)}, bf16[640,256]{1,0:T(8,128)(2,1)S(1)}, u32[]{:S(2)}, u32[]{:S(2)}) collective-permute-start(bf16[640,256]{1,0:T(8,128)(2,1)S(1)} %pad_maximum_fusion), channel_id=1, source_target_pairs={{0,64},{8,72},{16,80},{24,88},{32,96},{40,104},{48,112},{56,120},{... | collective-permute-start | bytes 983048 | tf_op jit(solution)/shard_map/ppermute | solution.py:473
  102.3 9.7 %collective-permute-start.9 = (bf16[320,256]{1,0:T(8,128)(2,1)S(1)}, bf16[320,256]{1,0:T(8,128)(2,1)S(1)}, u32[]{:S(2)}, u32[]{:S(2)}) collective-permute-start(bf16[320,256]{1,0:T(8,128)(2,1)S(1)} %fusion.7.kv_ref.rest_0_), channel_id=1, source_target_pairs={{0,32},{8,40},{16,48},{24,56},{32,0},{40,8},{48,16},{56,24},{64,96... | collective-permute-start | bytes 491528 | tf_op jit(solution)/shard_map/ppermute | solution.py:477
  112.0 14.6 %collective-permute-start.15 = (bf16[320,256]{1,0:T(8,128)(2,1)S(1)}, bf16[320,256]{1,0:T(8,128)(2,1)S(1)}, u32[]{:S(2)}, u32[]{:S(2)}) collective-permute-start(bf16[320,256]{1,0:T(8,128)(2,1)S(1)} %collective-permute-done.9.rest_2_), channel_id=1, source_target_pairs={{0,128},{8,136},{16,144},{24,152},{32,160},{40,168},{48,176},{56,1... | collective-permute-start | bytes 491528 | tf_op jit(solution)/shard_map/ppermute | solution.py:473
  112.7 13.9 %collective-permute-start.14 = (bf16[320,256]{1,0:T(8,128)(2,1)S(1)}, bf16[320,256]{1,0:T(8,128)(2,1)S(1)}, u32[]{:S(2)}, u32[]{:S(2)}) collective-permute-start(bf16[320,256]{1,0:T(8,128)(2,1)S(1)} %collective-permute-done.9.rest_2_), channel_id=1, source_target_pairs={{0,192},{8,200},{16,208},{24,216},{32,224},{40,232},{48,240},{56,2... | collective-permute-start | bytes 491528 | tf_op jit(solution)/shard_map/ppermute | solution.py:473
  115.4 11.3 %collective-permute-start.13 = (bf16[320,256]{1,0:T(8,128)(2,1)S(1)}, bf16[320,256]{1,0:T(8,128)(2,1)S(1)}, u32[]{:S(2)}, u32[]{:S(2)}) collective-permute-start(bf16[320,256]{1,0:T(8,128)(2,1)S(1)} %collective-permute-done.9.rest_2_), channel_id=1, source_target_pairs={{0,64},{8,72},{16,80},{24,88},{32,96},{40,104},{48,112},{56,120},{... | collective-permute-start | bytes 491528 | tf_op jit(solution)/shard_map/ppermute | solution.py:473
  132.4 6.2 %collective-permute-start.16 = (f32[136,1280]{1,0:T(8,128)S(1)}, f32[136,1280]{1,0:T(8,128)S(1)}, u32[]{:S(2)}, u32[]{:S(2)}) collective-permute-start(f32[136,1280]{1,0:T(8,128)S(1)} %get-tuple-element.55), channel_id=1, source_target_pairs={{0,8},{8,0},{16,24},{24,16},{32,40},{40,32},{48,56},{56,48},{64,72... | collective-permute-start | bytes 2088968 | tf_op jit(solution)/shard_map/ppermute | solution.py:481
  138.5 1.5 %collective-permute-start.17 = (bf16[320,256]{1,0:T(8,128)(2,1)S(1)}, bf16[320,256]{1,0:T(8,128)(2,1)S(1)}, u32[]{:S(2)}, u32[]{:S(2)}) collective-permute-start(bf16[320,256]{1,0:T(8,128)(2,1)S(1)} %get-tuple-element.57), channel_id=1, source_target_pairs={{0,8},{8,0},{16,24},{24,16},{32,40},{40,32},{48,56},{56,48},{64,72... | collective-permute-start | bytes 491528 | tf_op jit(solution)/shard_map/ppermute | solution.py:481
Sparse Core Ops, SparseCore 0:
  9.9 70.8 all-gather.1
